TPU v7x, 256 devices: a whole 4x4x8 slice. The times are simulated.
256 devices in a mesh: dp: 4 (over y_hi, core), ctx: 64 (over z, y_lo, x).
Axes of the slice: x: 4, y: 4 (y_hi: 2, y_lo: 2; y = y_hi * 2 + y_lo), z: 8, core: 2. Of those that a mesh axis runs over, the one named last changes fastest.
Arguments:
- hidden_states: bfloat16 [4, 8192, 1024], P('dp', 'ctx'), may hold values from -8 to 8
- short_weight: float32 [2, 3, 1024], replicated, may hold values from -3 to 3
- long_filter: bfloat16 [2, 512, 8192], P(None, 'ctx'), may hold values from -4 to 4
- cotangent: bfloat16 [4, 8192, 1024], P('dp', 'ctx'), may hold values from -0.03125 to 0.03125
Outputs:
- mixer_output: bfloat16 [4, 8192, 1024], P('dp', 'ctx')
- grad_filter: float32 [2, 512, 8192], P(None, 'ctx')
- grad_short: float32 [2, 3, 2, 512], P(None, None, None, 'ctx')
All inputs are finite; a program needn't handle non-finite values.
Results may differ from a plain program's by a relative error of at most 0.0057.
Values may be sent and summed in bfloat16 or wider, within the bound.
A program may use at most 64 MiB of HBM per device.

v0:
```python
import functools, math
import numpy as np, ml_dtypes
import jax, jax.numpy as jnp
from jax import lax
from jax.experimental import pallas as pl
from jax.experimental.pallas import tpu as pltpu

BF = jnp.bfloat16
F32 = jnp.float32
NB = 64
LN = 128
CH = 16


def split(x):
    hi = x.astype(ml_dtypes.bfloat16)
    lo = (x - hi.astype(np.float64)).astype(ml_dtypes.bfloat16)
    return hi, lo


def constants():
    n = 2 * NB * LN
    k1 = np.arange(NB)[:, None] + 0.5
    n1 = np.arange(NB)[None, :]
    th = 2 * np.pi * k1 * n1 / LN
    a = np.concatenate([np.cos(th), -np.sin(th)], 0)
    b = np.concatenate([np.cos(th.T), -np.sin(th.T)], 1) * (2.0 / n)
    tw = 2 * np.pi * k1 * np.arange(LN)[None, :] / n
    twc, tws = np.cos(tw), np.sin(tw)
    ph = 2 * np.pi * np.outer(np.arange(LN), np.arange(LN)) / LN
    c, s = np.cos(ph), np.sin(ph)
    m = np.block([[c, -s], [s, c]])
    mi = np.block([[c, s], [-s, c]])
    ah, al = split(a)
    bh, bl = split(b)
    mh, ml = split(m)
    ih, il = split(mi)
    amat = np.concatenate([ah, ah, al], 1)
    bmat = np.concatenate([bh, bl], 1)
    tws = np.stack([twc, tws]).astype(np.float32)
    mats = np.stack([mh, ml, ih, il])
    return amat, bmat, tws, mats


def dot(a, b):
    return jnp.dot(a, b, preferred_element_type=F32)


def hilo(x):
    hi = x.astype(BF)
    return hi, (x - hi.astype(F32)).astype(BF)


def row_f(f):
    return f if f < 8 else 23 - f


def rows_of(c):
    return pl.ds(c, NB, stride=CH)


def shift(x, k):
    m = x.shape[0] - 2
    lane = lax.broadcasted_iota(jnp.int32, (1, 1, LN), 2)
    if k == 0:
        return x[1:m + 1]
    if k > 0:
        r = pltpu.roll(x[0:m + 1], k, 2)
        return jnp.where(lane < k, r[0:m], r[1:m + 1])
    r = pltpu.roll(x[1:m + 2], LN + k, 2)
    return jnp.where(lane >= LN + k, r[1:m + 1], r[0:m])


def forward(src, spec, amat, tws, mats, zs, order, exact, precise):
    twc, tws_ = tws[0], tws[1]
    for pair in range(8):
        x = jnp.concatenate([src[rows_of(order[2 * pair]), :], src[rows_of(order[2 * pair + 1]), :]], 1)
        hi, lo = hilo(x)
        if exact:
            p = dot(amat[:, 64:192], jnp.concatenate([hi, hi], 0))
        else:
            p = dot(amat[...], jnp.concatenate([hi, lo, hi], 0))
        for h in range(2):
            re = p[0:64, h * LN:(h + 1) * LN]
            im = p[64:128, h * LN:(h + 1) * LN]
            z = jnp.concatenate([re * twc + im * tws_, im * twc - re * tws_], 1)
            zh, zl = hilo(z)
            r = (2 * pair + h) * NB
            zs[0, r:r + NB, :] = zh
            if precise > 1:
                zs[1, r:r + NB, :] = zl
    big(zs, spec, mats[0], mats[1], precise)


def big(zs, out, mh, ml, precise):
    for blk in range(4):
        rr = pl.ds(blk * 256, 256)
        zh = zs[0, rr, :]
        acc = dot(zh, mh)
        if precise > 0:
            acc = acc + dot(zh, ml)
        if precise > 1:
            acc = acc + dot(zs[1, rr, :], mh)
        out[rr, :] = acc


def put(zs, f, re, im, precise):
    z = jnp.concatenate([re, im], 1)
    zh, zl = hilo(z)
    zs[0, f * NB:(f + 1) * NB, :] = zh
    if precise > 1:
        zs[1, f * NB:(f + 1) * NB, :] = zl


def inverse(zs, tmp, dst, bmat, tws, mats, order, precise):
    big(zs, tmp, mats[2], mats[3], precise)
    twc, tws_ = tws[0], tws[1]
    for pair in range(8):
        us = []
        for h in range(2):
            r = (2 * pair + h) * NB
            re = tmp[r:r + NB, 0:LN]
            im = tmp[r:r + NB, LN:2 * LN]
            us.append(jnp.concatenate([re * twc - im * tws_, re * tws_ + im * twc], 0))
        u = jnp.concatenate(us, 1)
        uh, ul = hilo(u)
        y = dot(bmat[...], jnp.concatenate([uh, uh], 0))
        if precise > 1:
            y = y + dot(bmat[:, 0:128], ul)
        dst[rows_of(order[2 * pair]), :] = y[:, 0:LN]
        dst[rows_of(order[2 * pair + 1]), :] = y[:, LN:2 * LN]


def halves(ref, f):
    r = slice(f * NB, (f + 1) * NB)
    return ref[r, 0:LN], ref[r, LN:2 * LN]


def tap_rows(sw_ref, me, flipped, filter_order):
    row = lax.broadcasted_iota(jnp.int32, (CH, 1024), 0)
    lane = lax.broadcasted_iota(jnp.int32, (CH, 1024), 1)
    low = 8 * me + row
    if filter_order:
        high = 1023 - 8 * me - (row - 8)
    else:
        high = 1016 - 8 * me + (row - 8)
    chan = jnp.where(row < 8, low, high)
    if flipped:
        chan = 1023 - chan
    hit = lane == chan
    out = []
    for i in range(2):
        for k in range(3):
            w = sw_ref[i, k:k + 1, :]
            out.append(jnp.sum(jnp.where(hit, w, 0.0), axis=1, keepdims=True))
    return out


def wide(x):
    return jnp.broadcast_to(x, (CH, LN))[None]


STEP = 4
P_G, P_S, P_D, P_C, P_Q = 2, 1, 1, 1, 1

def kernel(recv, filt, sw, amat, bmat, tws, mats, out, gf, gs,
           xpad, fpad, qpad, buf, buf2, spec_s, spec_g, spec_d, tmp, zs):
    me = lax.axis_index("ctx")
    recv_order = list(range(CH))
    filt_order = list(range(CH))
    zero = jnp.zeros((CH, LN), F32)
    for p in (xpad, fpad, qpad):
        p[0] = zero
        p[NB + 1] = zero
    wf = [wide(w) for w in tap_rows(sw, me, False, True)]
    wn = [wide(w) for w in tap_rows(sw, me, False, False)]
    wr = [wide(w) for w in tap_rows(sw, me, True, False)]

    for i in range(NB):
        blk = filt[:, :, i * LN:(i + 1) * LN].astype(F32).reshape(CH, LN)
        fpad[i + 1] = blk

    def fold(i, _):
        x = fpad[pl.ds(i * STEP, STEP + 2)]
        g = wf[0] * shift(x, 0) + wf[1] * shift(x, 1) + wf[2] * shift(x, 2)
        buf[pl.ds(pl.multiple_of(i * STEP * CH, STEP * CH), STEP * CH), :] = g.reshape(STEP * CH, LN)
        return 0
    lax.fori_loop(0, NB // STEP, fold, 0)
    forward(buf, spec_g, amat, tws, mats, zs, filt_order, False, P_G)

    for i in range(NB):
        xpad[i + 1] = recv[i, 0:CH, :].astype(F32)
    xrows = xpad.reshape((NB + 2) * CH, LN)
    forward(xrows.at[pl.ds(CH, NB * CH)], spec_s, amat, tws, mats, zs, recv_order, True, P_S)

    for f in range(CH):
        r = row_f(f)
        gr, gi = halves(spec_g, f)
        sr, si = halves(spec_s, r)
        put(zs, r, gr * sr - gi * si, gr * si + gi * sr, P_C)
    inverse(zs, tmp, buf, bmat, tws, mats, recv_order, P_C)
    for f in range(CH):
        r = row_f(f)
        gr, gi = halves(spec_g, f)
        sr, si = halves(spec_s, 15 - r)
        put(zs, 15 - r, gr * sr + gi * si, gr * si - gi * sr, P_C)
    inverse(zs, tmp, buf2, bmat, tws, mats, recv_order, P_C)

    def gates(i, acc):
        x = xpad[pl.ds(i * STEP, STEP + 2)]
        xs = {k: shift(x, k) for k in range(-2, 3)}
        rr = pl.ds(pl.multiple_of(i * STEP * CH, STEP * CH), STEP * CH)
        cf = buf[rr, :].reshape(STEP, CH, LN)
        cr = buf2[rr, :].reshape(STEP, CH, LN)
        gatef = wn[3] * xs[0] + wn[4] * xs[1] + wn[5] * xs[2]
        gater = wr[3] * xs[0] + wr[4] * xs[-1] + wr[5] * xs[-2]
        mix = gatef * cf + gater * cr
        ct = recv[pl.ds(i * STEP, STEP), CH:2 * CH, :].astype(F32)
        out[pl.ds(i * STEP, STEP)] = mix.astype(BF)
        buf[rr, :] = (ct * gatef).reshape(STEP * CH, LN)
        buf2[rr, :] = (ct * gater).reshape(STEP * CH, LN)
        cf = cf * ct
        cr = cr * ct
        new = [jnp.sum(cf * xs[k], 0) for k in range(3)] + [jnp.sum(cr * xs[-k], 0) for k in range(3)]
        return tuple(a + b for a, b in zip(acc, new))
    acc = lax.fori_loop(0, NB // STEP, gates, (zero,) * 6)
    a_sum = [jnp.sum(a, 1, keepdims=True) for a in acc]

    forward(buf, spec_d, amat, tws, mats, zs, recv_order, False, P_D)
    forward(buf2, spec_g, amat, tws, mats, zs, recv_order, False, P_D)
    for f in range(CH):
        r = row_f(f)
        dr, di = halves(spec_d, r)
        sr, si = halves(spec_s, r)
        er, ei = halves(spec_g, 15 - r)
        tr, ti = halves(spec_s, 15 - r)
        put(zs, f, dr * sr + di * si + er * tr + ei * ti, di * sr - dr * si + er * ti - ei * tr, P_Q)
    inverse(zs, tmp, qpad.reshape((NB + 2) * CH, LN).at[pl.ds(CH, NB * CH)], bmat, tws, mats, filt_order, P_Q)

    def grads(i, acc):
        q = qpad[pl.ds(i * STEP, STEP + 2)]
        qs = [shift(q, -k) for k in range(3)]
        rr = pl.ds(pl.multiple_of(i * STEP * CH, STEP * CH), STEP * CH)
        fl = fpad[pl.ds(i * STEP + 1, STEP)]
        g = wf[0] * qs[0] + wf[1] * qs[1] + wf[2] * qs[2]
        buf[rr, :] = g.reshape(STEP * CH, LN)
        return tuple(a + jnp.sum(fl * qs[k], 0) for k, a in enumerate(acc))
    acc = lax.fori_loop(0, NB // STEP, grads, (zero,) * 3)
    for i in range(NB):
        gf[:, :, i * LN:(i + 1) * LN] = buf[i * CH:(i + 1) * CH, :].reshape(2, 8, LN)
    s0 = [jnp.sum(a, 1, keepdims=True) for a in acc]
    for k in range(3):
        gs[k] = jnp.broadcast_to(s0[k], (CH, LN))
        gs[3 + k] = jnp.broadcast_to(a_sum[k], (CH, LN))
        gs[6 + k] = jnp.broadcast_to(a_sum[3 + k], (CH, LN))


def run_kernel(recv, filt, sw):
    amat, bmat, tws, mats = constants()
    vm = pl.BlockSpec(memory_space=pltpu.VMEM)
    return pl.pallas_call(
        kernel,
        out_shape=(
            jax.ShapeDtypeStruct((NB, CH, LN), BF),
            jax.ShapeDtypeStruct((2, 8, NB * LN), F32),
            jax.ShapeDtypeStruct((9, CH, LN), F32),
        ),
        in_specs=[vm] * 7,
        out_specs=(vm,) * 3,
        scratch_shapes=[
            pltpu.VMEM((NB + 2, CH, LN), F32),
            pltpu.VMEM((NB + 2, CH, LN), F32),
            pltpu.VMEM((NB + 2, CH, LN), F32),
            pltpu.VMEM((NB * CH, LN), F32),
            pltpu.VMEM((NB * CH, LN), F32),
            pltpu.VMEM((CH * NB, 2 * LN), F32),
            pltpu.VMEM((CH * NB, 2 * LN), F32),
            pltpu.VMEM((CH * NB, 2 * LN), F32),
            pltpu.VMEM((CH * NB, 2 * LN), F32),
            pltpu.VMEM((2, CH * NB, 2 * LN), BF),
        ],
        compiler_params=pltpu.CompilerParams(vmem_limit_bytes=48 << 20),
    )(recv, filt, sw, jnp.asarray(amat), jnp.asarray(bmat), jnp.asarray(tws), jnp.asarray(mats))


def local(hidden, sw, filt, cot):
    x = hidden[0].astype(F32)
    scale = lax.rsqrt(jnp.mean(x * x, axis=1, keepdims=True) + 1e-06)
    normed = (x * scale).astype(BF)

    def chunk(a):
        a = a.T.reshape(128, 8, LN)
        return jnp.stack([a[:NB], a[NB:][::-1]], 1).reshape(NB, CH, LN)
    send = jnp.concatenate([chunk(normed), chunk(cot[0])], 1)
    recv = lax.all_to_all(send, "ctx", 0, 0, tiled=True)
    out, gf, gs = run_kernel(recv, filt, sw)
    back = lax.all_to_all(out, "ctx", 0, 0, tiled=True)
    back = back.reshape(NB, 2, 8, LN)
    chan = jnp.concatenate([back[:, 0].reshape(512, LN), back[::-1, 1].reshape(512, LN)], 0)
    gs = gs[:, :, 0].reshape(3, 3, CH)
    s0 = gs[0].reshape(3, 2, 8)
    a, b = gs[1], gs[2]
    s1 = jnp.stack([a[:, :8] + b[:, ::-1][:, :8], a[:, ::-1][:, :8] + b[:, :8]], 1)
    gf, gs = lax.psum((gf, jnp.stack([s0, s1])), "dp")
    return chan.T[None], gf, gs


def solution(mesh):
    from jax.sharding import PartitionSpec as P
    in_specs = (P("dp", "ctx", None), P(), P(None, "ctx", None), P("dp", "ctx", None))
    out_specs = (P("dp", "ctx", None), P(None, "ctx", None), P(None, None, None, "ctx"))
    return jax.shard_map(local, mesh=mesh, in_specs=in_specs, out_specs=out_specs, check_vma=False)
```

profile of v0, /device:TPU:1, one launch (start us, length us, event | category | flops | bytes accessed | tf_op | source)
XLA Modules:
  0.0 106.4 jit_solution(13703948213197040862)
XLA Ops:
  7.2 1.1 %copy.21 = bf16[1,128,1024]{1,2,0:T(8,128)(2,1)S(1)} copy(bf16[1,128,1024]{2,1,0:T(8,128)(2,1)} %param.8) | data formatting | bytes 524288 | tf_op args[0]
  8.3 0.2 fusion
  8.4 0.1 fusion.2
  8.6 0.9 copy-done.5
  9.5 0.2 copy.23
  9.7 0.1 copy_bitcast_fusion
  9.8 0.8 pad_maximum_fusion
  10.7 13.6 %all-to-all-start = ((bf16[64,32,128]{2,1,0:T(8,128)(2,1)}), bf16[64,32,128]{2,1,0:T(8,128)(2,1)S(1)}, u32[]{:S(2)}, u32[]{:S(2)}) async-start(bf16[64,32,128]{2,1,0:T(8,128)(2,1)} %pad_maximum_fusion), calls=%async_computation | async-start | bytes 1048576 | tf_op jit(solution)/shard_map/all_to_all | solution.py:295
  24.3 0.0 all-reduce.2.cloned.1.call-start
  24.4 15.7 %all-to-all-done.recv = bf16[64,32,128]{2,1,0:T(8,128)(2,1)S(1)} async-done(((bf16[64,32,128]{2,1,0:T(8,128)(2,1)}), bf16[64,32,128]{2,1,0:T(8,128)(2,1)S(1)}, u32[]{:S(2)}, u32[]{:S(2)}) %all-to-all-start) | async-done | bytes 524320 | tf_op jit(solution)/shard_map/all_to_all | solution.py:295
  40.1 10.1 %shard_map.103 = (bf16[64,16,128]{2,1,0:T(8,128)(2,1)}, f32[2,8,8192]{2,1,0:T(8,128)}, f32[9,16,128]{2,1,0:T(8,128)S(1)}) custom-call(bf16[64,32,128]{2,1,0:T(8,128)(2,1)S(1)} %all-to-all-done.recv, bf16[2,8,8192]{2,1,0:T(8,128)(2,1)S(1)} %copy-done.1, f32[2,3,1024]{2,1,0:T(4,128)S(1)} %copy.25.sw, bf16[128,192]{1,0:T(8,128)(2,1)S(1)} %copy-done.3, ...), custom_call_target="tpu_custom_call" | custom-call | tf_op jit(solution)/shard_map/pallas_call | solution.py:261
  50.2 0.1 slice_reduce_fusion.2
  50.3 0.1 slice.72
  50.4 0.1 slice.73
  50.5 7.0 %all-to-all-start.1 = ((bf16[64,16,128]{2,1,0:T(8,128)(2,1)}), bf16[64,16,128]{2,1,0:T(8,128)(2,1)S(1)}, u32[]{:S(2)}, u32[]{:S(2)}) async-start(bf16[64,16,128]{2,1,0:T(8,128)(2,1)} %get-tuple-element.6), calls=%async_computation.1 | async-start | bytes 524288 | tf_op jit(solution)/shard_map/all_to_all | solution.py:297
  57.5 0.1 add_bitcast_fusion.1
  57.6 0.1 stack_reshape_squeeze.3
  57.7 0.1 slice.75
  57.8 8.4 %psum.15 = f32[2,3,2,8]{3,2,0,1:T(2,128)S(1)} all-reduce(f32[2,3,2,8]{3,2,0,1:T(2,128)S(1)} %pad_maximum_fusion.3), channel_id=1, replica_groups=mesh['dp'=4,'ctx'=64] {'dp'}, use_global_device_ids=true, to_apply=%region_2.0 | all-reduce | flops 96 | bytes 768 | tf_op jit(solution)/shard_map/psum | solution.py:304
  66.3 0.6 copy.31
  66.9 1.3 %all-to-all-done.1 = bf16[64,16,128]{2,1,0:T(8,128)(2,1)S(1)} async-done(((bf16[64,16,128]{2,1,0:T(8,128)(2,1)}), bf16[64,16,128]{2,1,0:T(8,128)(2,1)S(1)}, u32[]{:S(2)}, u32[]{:S(2)}) %all-to-all-start.1) | async-done | bytes 262176 | tf_op jit(solution)/shard_map/all_to_all | solution.py:297
  68.2 0.9 copy.30
  69.0 28.6 %all-reduce.2.cloned.1.call-done = f32[2,8,8192]{2,1,0:T(8,128)} async-done(((f32[2,8,8192]{2,1,0:T(8,128)}), f32[2,8,8192]{2,1,0:T(8,128)}) %all-reduce.2.cloned.1.call-update) | async-done | bytes 524304 | tf_op jit(solution)/shard_map/psum | solution.py:304
  97.6 1.9 %copy.39 = f32[2,8,8192]{2,1,0:T(8,128)} copy(f32[2,8,8192]{2,1,0:T(8,128)} %all-reduce.2.cloned.1.call-done) | data formatting | bytes 1048576
  (27 shorter events, 0.2 us)
Async XLA Ops:
  8.5 1.0 copy-start.5
  10.7 13.7 %copy-start.6 = (f32[2,3,1024]{2,0,1:T(2,128)S(1)}, f32[2,3,1024]{2,0,1:T(2,128)}, u32[]{:S(2)}) copy-start(f32[2,3,1024]{2,0,1:T(2,128)} %param.9) | copy-start | bytes 73732
  10.7 29.4 %copy-start = (bf16[4,256,256]{2,1,0:T(8,128)(2,1)S(1)}, bf16[4,256,256]{2,1,0:T(8,128)(2,1)}, u32[]{:S(2)}) copy-start(bf16[4,256,256]{2,1,0:T(8,128)(2,1)} %constant.18.clone.mats) | copy-start | bytes 1572868
  10.7 29.4 %copy-start.1 = (bf16[2,8,8192]{2,1,0:T(8,128)(2,1)S(1)}, bf16[2,8,8192]{2,1,0:T(8,128)(2,1)}, u32[]{:S(2)}) copy-start(bf16[2,8,8192]{2,1,0:T(8,128)(2,1)} %filt.1) | copy-start | bytes 786436
  10.7 29.4 %copy-start.2 = (f32[2,64,128]{2,1,0:T(8,128)S(1)}, f32[2,64,128]{2,1,0:T(8,128)}, u32[]{:S(2)}) copy-start(f32[2,64,128]{2,1,0:T(8,128)} %constant.17.clone.tws) | copy-start | bytes 196612
  10.7 29.4 %copy-start.3 = (bf16[128,192]{1,0:T(8,128)(2,1)S(1)}, bf16[128,192]{1,0:T(8,128)(2,1)}, u32[]{:S(2)}) copy-start(bf16[128,192]{1,0:T(8,128)(2,1)} %constant.15.clone.amat) | copy-start | bytes 147460
  10.7 29.4 %all-to-all-start = ((bf16[64,32,128]{2,1,0:T(8,128)(2,1)}), bf16[64,32,128]{2,1,0:T(8,128)(2,1)S(1)}, u32[]{:S(2)}, u32[]{:S(2)}) async-start(bf16[64,32,128]{2,1,0:T(8,128)(2,1)} %pad_maximum_fusion), calls=%async_computation | async-start | bytes 1048576 | tf_op jit(solution)/shard_map/all_to_all | solution.py:295
  24.3 15.8 %copy-start.4 = (bf16[64,256]{1,0:T(8,128)(2,1)S(1)}, bf16[64,256]{1,0:T(8,128)(2,1)}, u32[]{:S(2)}) copy-start(bf16[64,256]{1,0:T(8,128)(2,1)} %constant.16.clone.bmat) | copy-start | bytes 98308
  24.3 73.3 %all-reduce.2.cloned.1.call-start = ((), (), s32[]{:S(2)}) async-start(), calls=%async_computation.2 | async-start | bytes 1048576 | tf_op jit(solution)/shard_map/psum | solution.py:304
  50.5 17.6 %all-to-all-start.1 = ((bf16[64,16,128]{2,1,0:T(8,128)(2,1)}), bf16[64,16,128]{2,1,0:T(8,128)(2,1)S(1)}, u32[]{:S(2)}, u32[]{:S(2)}) async-start(bf16[64,16,128]{2,1,0:T(8,128)(2,1)} %get-tuple-element.6), calls=%async_computation.1 | async-start | bytes 524288 | tf_op jit(solution)/shard_map/all_to_all | solution.py:297
Sparse Core Ops, SparseCore 0:
  50.3 47.2 all-reduce.1
where the time goes:
time: 107 us; the launch traced here: 106 us
  waiting for transfers between devices  45.5 us (43%)
  starting transfers between devices  20.7 us (19%)
  between operations  14.2 us (13%)
  Pallas kernels  10.1 us (9%)
  blocking collectives  8.44 us (8%)
  local copies, waits for them, and re-layouts  6.11 us (6%)
  other arithmetic  1.26 us (1%)
    psum x1, waiting for transfers between devices, local(): gf, gs = lax.psum((gf, jnp.stack([s0, s1])), 'dp')  28.6 us
    all_to_all x1, waiting for transfers between devices, local(): recv = lax.all_to_all(send, 'ctx', 0, 0, tiled=True)  15.7 us
    all_to_all x1, starting transfers between devices, local(): recv = lax.all_to_all(send, 'ctx', 0, 0, tiled=True)  13.6 us
    pallas_call x1, Pallas kernels, run_kernel(): pl.pallas_call(kernel, out_shape=(jax.ShapeDtypeStruct((NB, CH, LN), BF),...  10.1 us
    psum x1, blocking collectives, local(): gf, gs = lax.psum((gf, jnp.stack([s0, s1])), 'dp')  8.44 us
    all_to_all x1, starting transfers between devices, local(): back = lax.all_to_all(out, 'ctx', 0, 0, tiled=True)  7.04 us
    unnamed x20, local copies, waits for them, and re-layouts  5.57 us
  transfers between devices with their start and end apart: 3, of which 3 were waited for; matrix products, arithmetic and copies ran while one was open for 2% of the time, Pallas kernels for 0%

commit v1 on v0

--- a/solution.py
+++ b/solution.py
@@ -1,9 +1,9 @@
-import functools, math
 import numpy as np, ml_dtypes
 import jax, jax.numpy as jnp
 from jax import lax
 from jax.experimental import pallas as pl
 from jax.experimental.pallas import tpu as pltpu
+from jax.sharding import PartitionSpec as P
 
 BF = jnp.bfloat16
 F32 = jnp.float32
@@ -162,36 +162,95 @@
 
 STEP = 4
 P_G, P_S, P_D, P_C, P_Q = 2, 1, 1, 1, 1
-
-def kernel(recv, filt, sw, amat, bmat, tws, mats, out, gf, gs,
-           xpad, fpad, qpad, buf, buf2, spec_s, spec_g, spec_d, tmp, zs):
+MESH = pl.DeviceIdType.MESH
+
+
+def scatter(src, dst, send, recv):
     me = lax.axis_index("ctx")
+
+    def one(o, _):
+        q = lax.rem(me + o, NB)
+        pltpu.make_async_remote_copy(
+            src_ref=src.at[q], dst_ref=dst.at[me], send_sem=send, recv_sem=recv,
+            device_id={"ctx": q}, device_id_type=MESH).start()
+        return 0
+    lax.fori_loop(1, NB, one, 0)
+    dst[me] = src[me]
+
+
+def await_all(ref, sem):
+    part = ref.at[pl.ds(0, NB - 1)]
+    pltpu.make_async_copy(part, part, sem).wait()
+
+
+def to_chunks(get, dst):
+    for j in range(4):
+        low = get(j).T
+        high = get(7 - j).T
+        for g in range(16):
+            both = jnp.concatenate([low[8 * g:8 * g + 8], high[120 - 8 * g:128 - 8 * g]], 0)
+            dst[16 * j + g] = both.astype(BF)
+
+
+def kernel(hid, cot, filt, sw, amat, bmat, tws, mats, mixed, gf, gs,
+           sendx, sendc, recvx, recvc, sendo, recvo,
+           xpad, fpad, qpad, buf, buf2, spec_s, spec_g, spec_d, tmp, zs,
+           half_out, half_in, pair_out, pair_in, small_in,
+           sx, rx, sc, rc, so, ro, s2, r2):
+    me = lax.axis_index("ctx")
+    dp = lax.axis_index("dp")
+    core = lax.rem(dp, 2)
+    yhi = dp // 2
+    mate = yhi * 2 + 1 - core
+    far = (1 - yhi) * 2 + core
+    barrier = pltpu.get_barrier_semaphore()
+
+    def greet(o, _):
+        pl.semaphore_signal(barrier, inc=1, device_id={"ctx": lax.rem(me + o, NB)}, device_id_type=MESH)
+        return 0
+    lax.fori_loop(1, NB, greet, 0)
+    for o in range(1, 4):
+        pl.semaphore_signal(barrier, inc=1, device_id={"dp": lax.rem(dp + o, 4)}, device_id_type=MESH)
+
     recv_order = list(range(CH))
     filt_order = list(range(CH))
     zero = jnp.zeros((CH, LN), F32)
     for p in (xpad, fpad, qpad):
         p[0] = zero
         p[NB + 1] = zero
+
+    x = hid[...].astype(F32)
+    scale = lax.rsqrt(jnp.mean(x * x, axis=1, keepdims=True) + 1e-06)
+    to_chunks(lambda j: hid[:, j * LN:(j + 1) * LN].astype(F32) * scale, sendx)
+    pl.semaphore_wait(barrier, NB - 1 + 3)
+    scatter(sendx, recvx, sx, rx)
+    to_chunks(lambda j: cot[:, j * LN:(j + 1) * LN].astype(F32), sendc)
+    scatter(sendc, recvc, sc, rc)
+
     wf = [wide(w) for w in tap_rows(sw, me, False, True)]
     wn = [wide(w) for w in tap_rows(sw, me, False, False)]
     wr = [wide(w) for w in tap_rows(sw, me, True, False)]
 
     for i in range(NB):
-        blk = filt[:, :, i * LN:(i + 1) * LN].astype(F32).reshape(CH, LN)
-        fpad[i + 1] = blk
+        fpad[i + 1] = filt[:, :, i * LN:(i + 1) * LN].astype(F32).reshape(CH, LN)
+
+    def rows(i):
+        return pl.ds(pl.multiple_of(i * STEP * CH, STEP * CH), STEP * CH)
 
     def fold(i, _):
-        x = fpad[pl.ds(i * STEP, STEP + 2)]
-        g = wf[0] * shift(x, 0) + wf[1] * shift(x, 1) + wf[2] * shift(x, 2)
-        buf[pl.ds(pl.multiple_of(i * STEP * CH, STEP * CH), STEP * CH), :] = g.reshape(STEP * CH, LN)
+        v = fpad[pl.ds(i * STEP, STEP + 2)]
+        g = wf[0] * shift(v, 0) + wf[1] * shift(v, 1) + wf[2] * shift(v, 2)
+        buf[rows(i), :] = g.reshape(STEP * CH, LN)
         return 0
     lax.fori_loop(0, NB // STEP, fold, 0)
     forward(buf, spec_g, amat, tws, mats, zs, filt_order, False, P_G)
 
+    await_all(recvx, rx)
     for i in range(NB):
-        xpad[i + 1] = recv[i, 0:CH, :].astype(F32)
-    xrows = xpad.reshape((NB + 2) * CH, LN)
-    forward(xrows.at[pl.ds(CH, NB * CH)], spec_s, amat, tws, mats, zs, recv_order, True, P_S)
+        v = recvx[i].astype(F32)
+        xpad[i + 1] = v
+        buf[i * CH:(i + 1) * CH, :] = v
+    forward(buf, spec_s, amat, tws, mats, zs, recv_order, True, P_S)
 
     for f in range(CH):
         r = row_f(f)
@@ -206,25 +265,32 @@
         put(zs, 15 - r, gr * sr + gi * si, gr * si - gi * sr, P_C)
     inverse(zs, tmp, buf2, bmat, tws, mats, recv_order, P_C)
 
+    def mix(i, _):
+        v = xpad[pl.ds(i * STEP, STEP + 2)]
+        cf = buf[rows(i), :].reshape(STEP, CH, LN)
+        cr = buf2[rows(i), :].reshape(STEP, CH, LN)
+        gatef = wn[3] * shift(v, 0) + wn[4] * shift(v, 1) + wn[5] * shift(v, 2)
+        gater = wr[3] * shift(v, 0) + wr[4] * shift(v, -1) + wr[5] * shift(v, -2)
+        sendo[pl.ds(i * STEP, STEP)] = (gatef * cf + gater * cr).astype(BF)
+        return 0
+    lax.fori_loop(0, NB // STEP, mix, 0)
+    scatter(sendo, recvo, so, ro)
+
+    await_all(recvc, rc)
+
     def gates(i, acc):
-        x = xpad[pl.ds(i * STEP, STEP + 2)]
-        xs = {k: shift(x, k) for k in range(-2, 3)}
-        rr = pl.ds(pl.multiple_of(i * STEP * CH, STEP * CH), STEP * CH)
-        cf = buf[rr, :].reshape(STEP, CH, LN)
-        cr = buf2[rr, :].reshape(STEP, CH, LN)
+        v = xpad[pl.ds(i * STEP, STEP + 2)]
+        xs = {k: shift(v, k) for k in range(-2, 3)}
+        ct = recvc[pl.ds(i * STEP, STEP)].astype(F32)
+        cf = buf[rows(i), :].reshape(STEP, CH, LN) * ct
+        cr = buf2[rows(i), :].reshape(STEP, CH, LN) * ct
         gatef = wn[3] * xs[0] + wn[4] * xs[1] + wn[5] * xs[2]
         gater = wr[3] * xs[0] + wr[4] * xs[-1] + wr[5] * xs[-2]
-        mix = gatef * cf + gater * cr
-        ct = recv[pl.ds(i * STEP, STEP), CH:2 * CH, :].astype(F32)
-        out[pl.ds(i * STEP, STEP)] = mix.astype(BF)
-        buf[rr, :] = (ct * gatef).reshape(STEP * CH, LN)
-        buf2[rr, :] = (ct * gater).reshape(STEP * CH, LN)
-        cf = cf * ct
-        cr = cr * ct
+        buf[rows(i), :] = (ct * gatef).reshape(STEP * CH, LN)
+        buf2[rows(i), :] = (ct * gater).reshape(STEP * CH, LN)
         new = [jnp.sum(cf * xs[k], 0) for k in range(3)] + [jnp.sum(cr * xs[-k], 0) for k in range(3)]
         return tuple(a + b for a, b in zip(acc, new))
-    acc = lax.fori_loop(0, NB // STEP, gates, (zero,) * 6)
-    a_sum = [jnp.sum(a, 1, keepdims=True) for a in acc]
+    a_acc = lax.fori_loop(0, NB // STEP, gates, (zero,) * 6)
 
     forward(buf, spec_d, amat, tws, mats, zs, recv_order, False, P_D)
     forward(buf2, spec_g, amat, tws, mats, zs, recv_order, False, P_D)
@@ -235,78 +301,111 @@
         er, ei = halves(spec_g, 15 - r)
         tr, ti = halves(spec_s, 15 - r)
         put(zs, f, dr * sr + di * si + er * tr + ei * ti, di * sr - dr * si + er * ti - ei * tr, P_Q)
-    inverse(zs, tmp, qpad.reshape((NB + 2) * CH, LN).at[pl.ds(CH, NB * CH)], bmat, tws, mats, filt_order, P_Q)
+    inverse(zs, tmp, buf, bmat, tws, mats, filt_order, P_Q)
+    for i in range(NB):
+        qpad[i + 1] = buf[i * CH:(i + 1) * CH, :]
 
     def grads(i, acc):
-        q = qpad[pl.ds(i * STEP, STEP + 2)]
-        qs = [shift(q, -k) for k in range(3)]
-        rr = pl.ds(pl.multiple_of(i * STEP * CH, STEP * CH), STEP * CH)
+        v = qpad[pl.ds(i * STEP, STEP + 2)]
+        qs = [shift(v, -k) for k in range(3)]
         fl = fpad[pl.ds(i * STEP + 1, STEP)]
         g = wf[0] * qs[0] + wf[1] * qs[1] + wf[2] * qs[2]
-        buf[rr, :] = g.reshape(STEP * CH, LN)
+        half_out[0, pl.ds(i * STEP, STEP)] = g[:, 0:8]
+        half_out[1, pl.ds(i * STEP, STEP)] = g[:, 8:16]
         return tuple(a + jnp.sum(fl * qs[k], 0) for k, a in enumerate(acc))
-    acc = lax.fori_loop(0, NB // STEP, grads, (zero,) * 3)
-    for i in range(NB):
-        gf[:, :, i * LN:(i + 1) * LN] = buf[i * CH:(i + 1) * CH, :].reshape(2, 8, LN)
-    s0 = [jnp.sum(a, 1, keepdims=True) for a in acc]
-    for k in range(3):
-        gs[k] = jnp.broadcast_to(s0[k], (CH, LN))
-        gs[3 + k] = jnp.broadcast_to(a_sum[k], (CH, LN))
-        gs[6 + k] = jnp.broadcast_to(a_sum[3 + k], (CH, LN))
-
-
-def run_kernel(recv, filt, sw):
+    q_acc = lax.fori_loop(0, NB // STEP, grads, (zero,) * 3)
+
+    first = pltpu.make_async_remote_copy(
+        src_ref=half_out.at[1 - core], dst_ref=half_in, send_sem=s2.at[0], recv_sem=r2.at[0],
+        device_id={"dp": mate}, device_id_type=MESH)
+    first.start()
+    lane = lax.broadcasted_iota(jnp.int32, (CH, LN), 1)
+    small = zero
+    for k, a in enumerate(q_acc + a_acc):
+        small = jnp.where(lane == k, jnp.sum(a, 1, keepdims=True), small)
+    small_in[dp] = small
+    smalls = []
+    for o in range(1, 4):
+        c = pltpu.make_async_remote_copy(
+            src_ref=small_in.at[dp], dst_ref=small_in.at[dp], send_sem=s2.at[2 + o], recv_sem=r2.at[2 + o],
+            device_id={"dp": lax.rem(dp + o, 4)}, device_id_type=MESH)
+        c.start()
+        smalls.append(c)
+    first.wait()
+    for i in range(NB // 2):
+        a = half_out[core, 2 * i:2 * i + 2] + half_in[2 * i:2 * i + 2]
+        pair_out[i] = a.reshape(CH, LN).astype(BF)
+    second = pltpu.make_async_remote_copy(
+        src_ref=pair_out, dst_ref=pair_in, send_sem=s2.at[1], recv_sem=r2.at[1],
+        device_id={"dp": far}, device_id_type=MESH)
+    second.start()
+
+    await_all(recvo, ro)
+    for j in range(4):
+        low = jnp.concatenate([recvo[16 * j + g].astype(F32)[0:8] for g in range(16)], 0)
+        high = jnp.concatenate([recvo[16 * j + 15 - g].astype(F32)[8:16] for g in range(16)], 0)
+        mixed[:, j * LN:(j + 1) * LN] = low.T.astype(BF)
+        mixed[:, (7 - j) * LN:(8 - j) * LN] = high.T.astype(BF)
+
+    second.wait()
+    for i in range(NB // 2):
+        t = pair_out[i].astype(F32) + pair_in[i].astype(F32)
+        gf[core, :, 2 * i * LN:(2 * i + 1) * LN] = t[0:8]
+        gf[core, :, (2 * i + 1) * LN:(2 * i + 2) * LN] = t[8:16]
+    third = pltpu.make_async_remote_copy(
+        src_ref=gf.at[core], dst_ref=gf.at[core], send_sem=s2.at[2], recv_sem=r2.at[2],
+        device_id={"dp": mate}, device_id_type=MESH)
+    third.start()
+    for c in smalls:
+        c.wait()
+    gs[...] = (small_in[0] + small_in[1]) + (small_in[2] + small_in[3])
+    await_all(sendx, sx)
+    await_all(sendc, sc)
+    await_all(sendo, so)
+    third.wait()
+
+
+def run_kernel(hid, cot, filt, sw):
     amat, bmat, tws, mats = constants()
     vm = pl.BlockSpec(memory_space=pltpu.VMEM)
+    dma = pltpu.SemaphoreType.DMA
+    chunks = pltpu.VMEM((NB, CH, LN), BF)
+    padded = pltpu.VMEM((NB + 2, CH, LN), F32)
+    flat = pltpu.VMEM((NB * CH, LN), F32)
+    spec = pltpu.VMEM((CH * NB, 2 * LN), F32)
     return pl.pallas_call(
         kernel,
         out_shape=(
-            jax.ShapeDtypeStruct((NB, CH, LN), BF),
+            jax.ShapeDtypeStruct((LN, 1024), BF),
             jax.ShapeDtypeStruct((2, 8, NB * LN), F32),
-            jax.ShapeDtypeStruct((9, CH, LN), F32),
+            jax.ShapeDtypeStruct((CH, LN), F32),
         ),
-        in_specs=[vm] * 7,
+        in_specs=[vm] * 8,
         out_specs=(vm,) * 3,
-        scratch_shapes=[
-            pltpu.VMEM((NB + 2, CH, LN), F32),
-            pltpu.VMEM((NB + 2, CH, LN), F32),
-            pltpu.VMEM((NB + 2, CH, LN), F32),
-            pltpu.VMEM((NB * CH, LN), F32),
-            pltpu.VMEM((NB * CH, LN), F32),
-            pltpu.VMEM((CH * NB, 2 * LN), F32),
-            pltpu.VMEM((CH * NB, 2 * LN), F32),
-            pltpu.VMEM((CH * NB, 2 * LN), F32),
-            pltpu.VMEM((CH * NB, 2 * LN), F32),
+        scratch_shapes=[chunks] * 6 + [padded] * 3 + [flat] * 2 + [spec] * 4 + [
             pltpu.VMEM((2, CH * NB, 2 * LN), BF),
+            pltpu.VMEM((2, NB, 8, LN), F32),
+            pltpu.VMEM((NB, 8, LN), F32),
+            pltpu.VMEM((NB // 2, CH, LN), BF),
+            pltpu.VMEM((NB // 2, CH, LN), BF),
+            pltpu.VMEM((4, CH, LN), F32),
+            dma, dma, dma, dma, dma, dma, dma((6,)), dma((6,)),
         ],
-        compiler_params=pltpu.CompilerParams(vmem_limit_bytes=48 << 20),
-    )(recv, filt, sw, jnp.asarray(amat), jnp.asarray(bmat), jnp.asarray(tws), jnp.asarray(mats))
+        compiler_params=pltpu.CompilerParams(
+            vmem_limit_bytes=48 << 20, collective_id=0, has_side_effects=True),
+    )(hid, cot, filt, sw, jnp.asarray(amat), jnp.asarray(bmat), jnp.asarray(tws), jnp.asarray(mats))
 
 
 def local(hidden, sw, filt, cot):
-    x = hidden[0].astype(F32)
-    scale = lax.rsqrt(jnp.mean(x * x, axis=1, keepdims=True) + 1e-06)
-    normed = (x * scale).astype(BF)
-
-    def chunk(a):
-        a = a.T.reshape(128, 8, LN)
-        return jnp.stack([a[:NB], a[NB:][::-1]], 1).reshape(NB, CH, LN)
-    send = jnp.concatenate([chunk(normed), chunk(cot[0])], 1)
-    recv = lax.all_to_all(send, "ctx", 0, 0, tiled=True)
-    out, gf, gs = run_kernel(recv, filt, sw)
-    back = lax.all_to_all(out, "ctx", 0, 0, tiled=True)
-    back = back.reshape(NB, 2, 8, LN)
-    chan = jnp.concatenate([back[:, 0].reshape(512, LN), back[::-1, 1].reshape(512, LN)], 0)
-    gs = gs[:, :, 0].reshape(3, 3, CH)
+    mixed, gf, gs = run_kernel(hidden[0], cot[0], filt, sw)
+    gs = gs[:, :9].T.reshape(3, 3, CH)
+    a, b = gs[1], gs[2]
     s0 = gs[0].reshape(3, 2, 8)
-    a, b = gs[1], gs[2]
     s1 = jnp.stack([a[:, :8] + b[:, ::-1][:, :8], a[:, ::-1][:, :8] + b[:, :8]], 1)
-    gf, gs = lax.psum((gf, jnp.stack([s0, s1])), "dp")
-    return chan.T[None], gf, gs
+    return mixed[None], gf, jnp.stack([s0, s1])
 
 
 def solution(mesh):
-    from jax.sharding import PartitionSpec as P
     in_specs = (P("dp", "ctx", None), P(), P(None, "ctx", None), P("dp", "ctx", None))
     out_specs = (P("dp", "ctx", None), P(None, "ctx", None), P(None, None, None, "ctx"))
     return jax.shard_map(local, mesh=mesh, in_specs=in_specs, out_specs=out_specs, check_vma=False)

time: 107 us -> 50.1 us (0.47)
  waiting for transfers between devices: 45.5 us -> 0 us
  Pallas kernels: 10.1 us -> 40.1 us
  starting transfers between devices: 20.7 us -> 0 us
  between operations: 14.2 us -> 0.69 us
  blocking collectives: 8.44 us -> 0 us
  local copies, waits for them, and re-layouts: 6.11 us -> 8.17 us
    pallas_call x1, Pallas kernels: 10.1 us -> 40.1 us  [run_kernel(): pl.pallas_call(kernel, out_shape=(jax.ShapeDtypeStruct((LN, 1024), BF), j...]
    psum x1 -> x0, waiting for transfers between devices: 28.6 us -> none  [local(): gf, gs = lax.psum((gf, jnp.stack([s0, s1])), 'dp')]
    all_to_all x2 -> x0, starting transfers between devices: 20.7 us -> none  [the longest x1 13.6 us: local(): recv = lax.all_to_all(send, 'ctx', 0, 0, tiled=True)]
    all_to_all x2 -> x0, waiting for transfers between devices: 16.9 us -> none  [the longest x1 15.7 us: local(): recv = lax.all_to_all(send, 'ctx', 0, 0, tiled=True)]
    psum x1 -> x0, blocking collectives: 8.44 us -> none  [local(): gf, gs = lax.psum((gf, jnp.stack([s0, s1])), 'dp')]
    unnamed x20 -> x17, local copies, waits for them, and re-layouts: 5.57 us -> 7.82 us
  transfers between devices with their start and end apart: 3 -> 0, of which waited for: 3 -> 0; matrix products, arithmetic and copies ran while one was open for 2% -> 0% of each run, Pallas kernels for 0% -> 0%
where the time goes in v1:
time: 50.1 us; the launch traced here: 49.7 us
  Pallas kernels  40.1 us (80%)
  local copies, waits for them, and re-layouts  8.17 us (16%)
  other arithmetic  0.69 us (1%)
  between operations  0.69 us (1%)
    pallas_call x1, Pallas kernels, run_kernel(): pl.pallas_call(kernel, out_shape=(jax.ShapeDtypeStruct((LN, 1024), BF), j...  40.1 us
    unnamed x17, local copies, waits for them, and re-layouts  7.82 us

profile of v1, /device:TPU:1, one launch (start us, length us, event | category | flops | bytes accessed | tf_op | source)
XLA Modules:
  0.0 49.7 jit_solution(2125683980040410042)
XLA Ops:
  0.6 0.0 copy-start.6
  0.6 0.8 %copy.11.sw = f32[2,3,1024]{2,1,0:T(4,128)S(1)} copy(f32[2,3,1024]{2,0,1:T(2,128)} %param.9) | data formatting | bytes 49152 | tf_op args[1]
  1.4 0.0 copy-done.6
  1.4 0.0 copy-start
  1.4 1.0 %copy-done = bf16[4,256,256]{2,1,0:T(8,128)(2,1)S(1)} copy-done((bf16[4,256,256]{2,1,0:T(8,128)(2,1)S(1)}, bf16[4,256,256]{2,1,0:T(8,128)(2,1)}, u32[]{:S(2)}) %copy-start) | copy-done | bytes 524312
  2.5 0.0 copy-start.1
  2.5 0.9 %copy-done.1 = bf16[1,128,1024]{2,1,0:T(8,128)(2,1)S(1)} copy-done((bf16[1,128,1024]{2,1,0:T(8,128)(2,1)S(1)}, bf16[1,128,1024]{2,1,0:T(8,128)(2,1)}, u32[]{:S(2)}) %copy-start.1) | copy-done | bytes 262168
  3.4 0.0 copy-start.2
  3.4 0.9 %copy-done.2 = bf16[1,128,1024]{2,1,0:T(8,128)(2,1)S(1)} copy-done((bf16[1,128,1024]{2,1,0:T(8,128)(2,1)S(1)}, bf16[1,128,1024]{2,1,0:T(8,128)(2,1)}, u32[]{:S(2)}) %copy-start.2) | copy-done | bytes 262168
  4.4 0.0 copy-start.3
  4.4 0.9 %copy-done.3 = bf16[2,8,8192]{2,1,0:T(8,128)(2,1)S(1)} copy-done((bf16[2,8,8192]{2,1,0:T(8,128)(2,1)S(1)}, bf16[2,8,8192]{2,1,0:T(8,128)(2,1)}, u32[]{:S(2)}) %copy-start.3) | copy-done | bytes 262168
  5.3 0.0 copy-start.4
  5.3 0.8 %copy-done.4 = f32[2,64,128]{2,1,0:T(8,128)S(1)} copy-done((f32[2,64,128]{2,1,0:T(8,128)S(1)}, f32[2,64,128]{2,1,0:T(8,128)}, u32[]{:S(2)}) %copy-start.4) | copy-done | bytes 65560
  6.2 0.0 copy-start.5
  6.2 0.8 %copy-done.5 = bf16[128,192]{1,0:T(8,128)(2,1)S(1)} copy-done((bf16[128,192]{1,0:T(8,128)(2,1)S(1)}, bf16[128,192]{1,0:T(8,128)(2,1)}, u32[]{:S(2)}) %copy-start.5) | copy-done | bytes 49176
  7.0 40.1 %shard_map.103 = (bf16[128,1024]{1,0:T(8,128)(2,1)S(1)}, f32[2,8,8192]{2,1,0:T(8,128)S(1)}, f32[16,128]{1,0:T(8,128)S(1)}) custom-call(bf16[128,1024]{1,0:T(8,128)(2,1)S(1)} %bitcast.13, bf16[128,1024]{1,0:T(8,128)(2,1)S(1)} %bitcast.14, bf16[2,8,8192]{2,1,0:T(8,128)(2,1)S(1)} %copy-done.3, f32[2,3,1024]{2,1,0:T(4,128)S(1)} %copy.11.sw, ...), custom_call_target="tpu_custom_call" | custom-call | tf_op jit(solution)/shard_map/pallas_call | solution.py:376
  47.1 0.1 copy.16
  47.2 0.1 fusion
  47.3 0.1 slice_add_fusion.1
  47.4 0.1 copy.13
  47.5 0.1 copy.14
  47.6 0.6 %pad_maximum_fusion = f32[2,3,2,8]{3,2,1,0:T(2,128)} fusion(f32[1,3,2,8]{3,2,1,0:T(2,128)S(1)} %bitcast.15, f32[1,3,2,8]{3,2,1,0:T(2,128)S(1)} %copy.16), kind=kLoop, calls=%fused_computation.2 | loop fusion | flops 96 | bytes 768 | tf_op jit(solution)/shard_map/stack | solution.py:405
  48.2 0.7 %copy.21 = bf16[1,128,1024]{2,1,0:T(8,128)(2,1)} copy(bf16[1,128,1024]{2,1,0:T(8,128)(2,1)S(1)} %bitcast.12) | data formatting | bytes 524288
  48.9 0.8 %copy.22 = f32[2,8,8192]{2,1,0:T(8,128)} copy(f32[2,8,8192]{2,1,0:T(8,128)S(1)} %get-tuple-element.17) | data formatting | bytes 1048576
  (6 shorter events, 0.0 us)
Async XLA Ops:
  0.6 0.8 %copy-start.6 = (bf16[64,256]{1,0:T(8,128)(2,1)S(1)}, bf16[64,256]{1,0:T(8,128)(2,1)}, u32[]{:S(2)}) copy-start(bf16[64,256]{1,0:T(8,128)(2,1)} %constant.9.clone.bmat) | copy-start | bytes 98308
  1.4 1.0 %copy-start = (bf16[4,256,256]{2,1,0:T(8,128)(2,1)S(1)}, bf16[4,256,256]{2,1,0:T(8,128)(2,1)}, u32[]{:S(2)}) copy-start(bf16[4,256,256]{2,1,0:T(8,128)(2,1)} %constant.11.clone.mats) | copy-start | bytes 1572868
  2.5 0.9 %copy-start.1 = (bf16[1,128,1024]{2,1,0:T(8,128)(2,1)S(1)}, bf16[1,128,1024]{2,1,0:T(8,128)(2,1)}, u32[]{:S(2)}) copy-start(bf16[1,128,1024]{2,1,0:T(8,128)(2,1)} %param.8) | copy-start | bytes 786436
  3.4 0.9 %copy-start.2 = (bf16[1,128,1024]{2,1,0:T(8,128)(2,1)S(1)}, bf16[1,128,1024]{2,1,0:T(8,128)(2,1)}, u32[]{:S(2)}) copy-start(bf16[1,128,1024]{2,1,0:T(8,128)(2,1)} %param.11) | copy-start | bytes 786436
  4.4 0.9 %copy-start.3 = (bf16[2,8,8192]{2,1,0:T(8,128)(2,1)S(1)}, bf16[2,8,8192]{2,1,0:T(8,128)(2,1)}, u32[]{:S(2)}) copy-start(bf16[2,8,8192]{2,1,0:T(8,128)(2,1)} %filt.1) | copy-start | bytes 786436
  5.3 0.8 %copy-start.4 = (f32[2,64,128]{2,1,0:T(8,128)S(1)}, f32[2,64,128]{2,1,0:T(8,128)}, u32[]{:S(2)}) copy-start(f32[2,64,128]{2,1,0:T(8,128)} %constant.10.clone.tws) | copy-start | bytes 196612
  6.2 0.8 %copy-start.5 = (bf16[128,192]{1,0:T(8,128)(2,1)S(1)}, bf16[128,192]{1,0:T(8,128)(2,1)}, u32[]{:S(2)}) copy-start(bf16[128,192]{1,0:T(8,128)(2,1)} %constant.8.clone.amat) | copy-start | bytes 147460

commit v2 on v1

--- a/solution.py
+++ b/solution.py
@@ -151,7 +151,7 @@
     out = []
     for i in range(2):
         for k in range(3):
-            w = sw_ref[i, k:k + 1, :]
+            w = sw_ref[k, i:i + 1, :]
             out.append(jnp.sum(jnp.where(hit, w, 0.0), axis=1, keepdims=True))
     return out
 
@@ -192,11 +192,16 @@
             dst[16 * j + g] = both.astype(BF)
 
 
-def kernel(hid, cot, filt, sw, amat, bmat, tws, mats, mixed, gf, gs,
+def kernel(hid_h, cot_h, filt_h, sw_h, amat_h, bmat_h, tws_h, mats_h, mixed, gf, gs,
+           hid, cot, filt, sw, amat, bmat, tws, mats,
            sendx, sendc, recvx, recvc, sendo, recvo,
            xpad, fpad, qpad, buf, buf2, spec_s, spec_g, spec_d, tmp, zs,
            half_out, half_in, pair_out, pair_in, small_in,
-           sx, rx, sc, rc, so, ro, s2, r2):
+           sx, rx, sc, rc, so, ro, s2, r2, ins):
+    pairs = ((hid_h, hid), (cot_h, cot), (filt_h, filt), (sw_h, sw), (amat_h, amat), (bmat_h, bmat), (tws_h, tws), (mats_h, mats))
+    loads = [pltpu.make_async_copy(a, b, ins.at[i]) for i, (a, b) in enumerate(pairs)]
+    for c in loads:
+        c.start()
     me = lax.axis_index("ctx")
     dp = lax.axis_index("dp")
     core = lax.rem(dp, 2)
@@ -219,14 +224,18 @@
         p[0] = zero
         p[NB + 1] = zero
 
+    loads[0].wait()
     x = hid[...].astype(F32)
     scale = lax.rsqrt(jnp.mean(x * x, axis=1, keepdims=True) + 1e-06)
     to_chunks(lambda j: hid[:, j * LN:(j + 1) * LN].astype(F32) * scale, sendx)
     pl.semaphore_wait(barrier, NB - 1 + 3)
     scatter(sendx, recvx, sx, rx)
+    loads[1].wait()
     to_chunks(lambda j: cot[:, j * LN:(j + 1) * LN].astype(F32), sendc)
     scatter(sendc, recvc, sc, rc)
 
+    for c in loads[2:]:
+        c.wait()
     wf = [wide(w) for w in tap_rows(sw, me, False, True)]
     wn = [wide(w) for w in tap_rows(sw, me, False, False)]
     wr = [wide(w) for w in tap_rows(sw, me, True, False)]
@@ -242,7 +251,7 @@
         g = wf[0] * shift(v, 0) + wf[1] * shift(v, 1) + wf[2] * shift(v, 2)
         buf[rows(i), :] = g.reshape(STEP * CH, LN)
         return 0
-    lax.fori_loop(0, NB // STEP, fold, 0)
+    lax.fori_loop(0, NB // STEP, fold, 0, unroll=NB // STEP)
     forward(buf, spec_g, amat, tws, mats, zs, filt_order, False, P_G)
 
     await_all(recvx, rx)
@@ -273,7 +282,7 @@
         gater = wr[3] * shift(v, 0) + wr[4] * shift(v, -1) + wr[5] * shift(v, -2)
         sendo[pl.ds(i * STEP, STEP)] = (gatef * cf + gater * cr).astype(BF)
         return 0
-    lax.fori_loop(0, NB // STEP, mix, 0)
+    lax.fori_loop(0, NB // STEP, mix, 0, unroll=NB // STEP)
     scatter(sendo, recvo, so, ro)
 
     await_all(recvc, rc)
@@ -290,7 +299,7 @@
         buf2[rows(i), :] = (ct * gater).reshape(STEP * CH, LN)
         new = [jnp.sum(cf * xs[k], 0) for k in range(3)] + [jnp.sum(cr * xs[-k], 0) for k in range(3)]
         return tuple(a + b for a, b in zip(acc, new))
-    a_acc = lax.fori_loop(0, NB // STEP, gates, (zero,) * 6)
+    a_acc = lax.fori_loop(0, NB // STEP, gates, (zero,) * 6, unroll=NB // STEP)
 
     forward(buf, spec_d, amat, tws, mats, zs, recv_order, False, P_D)
     forward(buf2, spec_g, amat, tws, mats, zs, recv_order, False, P_D)
@@ -313,7 +322,7 @@
         half_out[0, pl.ds(i * STEP, STEP)] = g[:, 0:8]
         half_out[1, pl.ds(i * STEP, STEP)] = g[:, 8:16]
         return tuple(a + jnp.sum(fl * qs[k], 0) for k, a in enumerate(acc))
-    q_acc = lax.fori_loop(0, NB // STEP, grads, (zero,) * 3)
+    q_acc = lax.fori_loop(0, NB // STEP, grads, (zero,) * 3, unroll=NB // STEP)
 
     first = pltpu.make_async_remote_copy(
         src_ref=half_out.at[1 - core], dst_ref=half_in, send_sem=s2.at[0], recv_sem=r2.at[0],
@@ -358,7 +367,16 @@
     third.start()
     for c in smalls:
         c.wait()
-    gs[...] = (small_in[0] + small_in[1]) + (small_in[2] + small_in[3])
+    total = (small_in[0] + small_in[1]) + (small_in[2] + small_in[3])
+    row = lax.broadcasted_iota(jnp.int32, (CH, LN), 0)
+
+    def flat_rows(item, target):
+        return jnp.sum(jnp.where(row == target, total[:, item:item + 1], 0.0), 0, keepdims=True)[:, 0:8]
+    for k in range(3):
+        gs[0, k] = jnp.concatenate([flat_rows(k, lane), flat_rows(k, lane + 8)], 0)
+        gs[1, k] = jnp.concatenate([
+            flat_rows(3 + k, lane) + flat_rows(6 + k, 15 - lane),
+            flat_rows(3 + k, 15 - lane) + flat_rows(6 + k, lane)], 0)
     await_all(sendx, sx)
     await_all(sendc, sc)
     await_all(sendo, so)
@@ -373,36 +391,34 @@
     padded = pltpu.VMEM((NB + 2, CH, LN), F32)
     flat = pltpu.VMEM((NB * CH, LN), F32)
     spec = pltpu.VMEM((CH * NB, 2 * LN), F32)
+    ops = (hid, cot, filt, sw, jnp.asarray(amat), jnp.asarray(bmat), jnp.asarray(tws), jnp.asarray(mats))
+    held = [pltpu.VMEM(a.shape, a.dtype) for a in ops]
     return pl.pallas_call(
         kernel,
         out_shape=(
-            jax.ShapeDtypeStruct((LN, 1024), BF),
-            jax.ShapeDtypeStruct((2, 8, NB * LN), F32),
-            jax.ShapeDtypeStruct((CH, LN), F32),
+            pltpu.VMEM((LN, 1024), BF),
+            pltpu.VMEM((2, 8, NB * LN), F32),
+            pltpu.VMEM((2, 3, 2, 8), F32),
         ),
-        in_specs=[vm] * 8,
+        in_specs=[pl.BlockSpec(memory_space=pltpu.HBM)] * 8,
         out_specs=(vm,) * 3,
-        scratch_shapes=[chunks] * 6 + [padded] * 3 + [flat] * 2 + [spec] * 4 + [
+        scratch_shapes=held + [chunks] * 6 + [padded] * 3 + [flat] * 2 + [spec] * 4 + [
             pltpu.VMEM((2, CH * NB, 2 * LN), BF),
             pltpu.VMEM((2, NB, 8, LN), F32),
             pltpu.VMEM((NB, 8, LN), F32),
             pltpu.VMEM((NB // 2, CH, LN), BF),
             pltpu.VMEM((NB // 2, CH, LN), BF),
             pltpu.VMEM((4, CH, LN), F32),
-            dma, dma, dma, dma, dma, dma, dma((6,)), dma((6,)),
+            dma, dma, dma, dma, dma, dma, dma((6,)), dma((6,)), dma((8,)),
         ],
         compiler_params=pltpu.CompilerParams(
-            vmem_limit_bytes=48 << 20, collective_id=0, has_side_effects=True),
-    )(hid, cot, filt, sw, jnp.asarray(amat), jnp.asarray(bmat), jnp.asarray(tws), jnp.asarray(mats))
+            vmem_limit_bytes=57 << 20, collective_id=0, has_side_effects=True),
+    )(*ops)
 
 
 def local(hidden, sw, filt, cot):
-    mixed, gf, gs = run_kernel(hidden[0], cot[0], filt, sw)
-    gs = gs[:, :9].T.reshape(3, 3, CH)
-    a, b = gs[1], gs[2]
-    s0 = gs[0].reshape(3, 2, 8)
-    s1 = jnp.stack([a[:, :8] + b[:, ::-1][:, :8], a[:, ::-1][:, :8] + b[:, :8]], 1)
-    return mixed[None], gf, jnp.stack([s0, s1])
+    mixed, gf, gs = run_kernel(hidden[0], cot[0], filt, jnp.swapaxes(sw, 0, 1))
+    return mixed[None], gf, gs
 
 
 def solution(mesh):

time: 50.1 us -> 41.3 us (0.82)
  local copies, waits for them, and re-layouts: 8.17 us -> 2.09 us
  Pallas kernels: 40.1 us -> 38.5 us
  other arithmetic: 0.69 us -> 0 us
    unnamed x17 -> x3, local copies, waits for them, and re-layouts: 7.82 us -> 2.09 us
    pallas_call x1, Pallas kernels: 40.1 us -> 38.5 us  [run_kernel(): pl.pallas_call(kernel, out_shape=(pltpu.VMEM((LN, 1024), BF), pltpu.VMEM(...]
    another operation x2 -> x0, other arithmetic: 0.61 us -> none  [the longest x1 0.6 us: local(): return (mixed[None], gf, jnp.stack([s0, s1]))]
where the time goes in v2:
time: 41.3 us; the launch traced here: 41.2 us
  Pallas kernels  38.5 us (93%)
  local copies, waits for them, and re-layouts  2.09 us (5%)
  between operations  0.64 us (2%)
    pallas_call x1, Pallas kernels, run_kernel(): pl.pallas_call(kernel, out_shape=(pltpu.VMEM((LN, 1024), BF), pltpu.VMEM(...  38.5 us
    unnamed x3, local copies, waits for them, and re-layouts  2.09 us

profile of v2, /device:TPU:1, one launch (start us, length us, event | category | flops | bytes accessed | tf_op | source)
XLA Modules:
  0.0 41.2 jit_solution(15872779312611465477)
XLA Ops:
  0.6 38.5 %shard_map.103 = (bf16[128,1024]{1,0:T(8,128)(2,1)S(1)}, f32[2,8,8192]{2,1,0:T(8,128)S(1)}, f32[2,3,2,8]{3,2,1,0:T(2,128)S(1)}) custom-call(bf16[128,1024]{1,0:T(8,128)(2,1)} %bitcast.5, bf16[128,1024]{1,0:T(8,128)(2,1)} %bitcast.6, bf16[2,8,8192]{2,1,0:T(8,128)(2,1)} %filt_h.1, f32[3,2,1024]{2,1,0:T(2,128)} %bitcast.7, ...), custom_call_target="tpu_custom_call" | custom-call | tf_op jit(solution)/shard_map/pallas_call | solution.py:396
  39.1 0.7 %copy.14 = bf16[1,128,1024]{2,1,0:T(8,128)(2,1)} copy(bf16[1,128,1024]{2,1,0:T(8,128)(2,1)S(1)} %bitcast.4) | data formatting | bytes 524288
  39.9 0.6 %copy.16 = f32[2,3,2,8]{3,2,1,0:T(2,128)} copy(f32[2,3,2,8]{3,2,1,0:T(2,128)S(1)} %get-tuple-element.11) | data formatting | bytes 768
  40.4 0.8 %copy.15 = f32[2,8,8192]{2,1,0:T(8,128)} copy(f32[2,8,8192]{2,1,0:T(8,128)S(1)} %get-tuple-element.10) | data formatting | bytes 1048576

commit v3 on v2

v3 whole, which is shorter than its diff:
```python
import functools

import numpy as np, ml_dtypes
import jax, jax.numpy as jnp
from jax import lax
from jax.experimental import pallas as pl
from jax.experimental.pallas import tpu as pltpu
from jax.sharding import PartitionSpec as P

BF = jnp.bfloat16
F32 = jnp.float32
NB = 64
LN = 128
CH = 16


def split(x):
    hi = x.astype(ml_dtypes.bfloat16)
    lo = (x - hi.astype(np.float64)).astype(ml_dtypes.bfloat16)
    return hi, lo


def constants():
    n = 2 * NB * LN
    k1 = np.arange(NB)[:, None] + 0.5
    n1 = np.arange(NB)[None, :]
    th = 2 * np.pi * k1 * n1 / LN
    a = np.concatenate([np.cos(th), -np.sin(th)], 0)
    b = np.concatenate([np.cos(th.T), -np.sin(th.T)], 1) * (2.0 / n)
    tw = 2 * np.pi * k1 * np.arange(LN)[None, :] / n
    twc, tws = np.cos(tw), np.sin(tw)
    ph = 2 * np.pi * np.outer(np.arange(LN), np.arange(LN)) / LN
    c, s = np.cos(ph), np.sin(ph)
    m = np.block([[c, -s], [s, c]])
    mi = np.block([[c, s], [-s, c]])
    ah, al = split(a)
    bh, bl = split(b)
    mh, ml = split(m)
    ih, il = split(mi)
    amat = np.concatenate([ah, ah, al], 1)
    bmat = np.concatenate([bh, bl], 1)
    tws = np.stack([twc, tws]).astype(np.float32)
    mats = np.stack([mh, ml, ih, il])
    return amat, bmat, tws, mats


def dot(a, b):
    return jnp.dot(a, b, preferred_element_type=F32)


def hilo(x):
    hi = x.astype(BF)
    return hi, (x - hi.astype(F32)).astype(BF)


def row_f(f):
    return f if f < 8 else 23 - f


def column(c, base=0, stride=CH):
    return pl.ds(base + c, NB, stride=stride)


def shift(x, k):
    m = x.shape[0] - 2
    lane = lax.broadcasted_iota(jnp.int32, (1, 1, LN), 2)
    if k == 0:
        return x[1:m + 1]
    if k > 0:
        r = pltpu.roll(x[0:m + 1], k, 2)
        return jnp.where(lane < k, r[0:m], r[1:m + 1])
    r = pltpu.roll(x[1:m + 2], LN + k, 2)
    return jnp.where(lane >= LN + k, r[1:m + 1], r[0:m])


def forward(src, base, spec, amat, tws, mats, zs, slot, chans, exact, precise):
    twc, tws_ = tws[0], tws[1]
    for pair in range(len(chans) // 2):
        x = jnp.concatenate([src[column(c, base), :] for c in chans[2 * pair:2 * pair + 2]], 1)
        hi, lo = hilo(x)
        if exact:
            p = dot(amat[:, 64:192], jnp.concatenate([hi, hi], 0))
        else:
            p = dot(amat[...], jnp.concatenate([hi, lo, hi], 0))
        for h in range(2):
            re = p[0:64, h * LN:(h + 1) * LN]
            im = p[64:128, h * LN:(h + 1) * LN]
            put(zs, slot + 2 * pair + h, re * twc + im * tws_, im * twc - re * tws_, precise)
    big(zs, slot * NB, spec, chans[0] * NB, len(chans) * NB, mats[0], mats[1], precise)


def big(zs, at, out, to, rows, mh, ml, precise):
    for r in range(0, rows, 256):
        zh = zs[0, at + r:at + r + 256, :]
        acc = dot(zh, mh)
        if precise > 0:
            acc = acc + dot(zh, ml)
        if precise > 1:
            acc = acc + dot(zs[1, at + r:at + r + 256, :], mh)
        out[to + r:to + r + 256, :] = acc


def put(zs, f, re, im, precise):
    z = jnp.concatenate([re, im], 1)
    zh, zl = hilo(z)
    zs[0, f * NB:(f + 1) * NB, :] = zh
    if precise > 1:
        zs[1, f * NB:(f + 1) * NB, :] = zl


def inverse(zs, slot, count, tmp, bmat, tws, mats, precise, store):
    big(zs, slot * NB, tmp, slot * NB, count * NB, mats[2], mats[3], precise)
    twc, tws_ = tws[0], tws[1]
    for pair in range(count // 2):
        us = []
        for h in range(2):
            r = (slot + 2 * pair + h) * NB
            re = tmp[r:r + NB, 0:LN]
            im = tmp[r:r + NB, LN:2 * LN]
            us.append(jnp.concatenate([re * twc - im * tws_, re * tws_ + im * twc], 0))
        u = jnp.concatenate(us, 1)
        uh, ul = hilo(u)
        y = dot(bmat[...], jnp.concatenate([uh, uh], 0))
        if precise > 1:
            y = y + dot(bmat[:, 0:128], ul)
        store(slot + 2 * pair, y[:, 0:LN])
        store(slot + 2 * pair + 1, y[:, LN:2 * LN])


def halves(ref, f):
    r = slice(f * NB, (f + 1) * NB)
    return ref[r, 0:LN], ref[r, LN:2 * LN]


def tap_rows(sw_ref, me, flipped, filter_order):
    row = lax.broadcasted_iota(jnp.int32, (CH, 1024), 0)
    lane = lax.broadcasted_iota(jnp.int32, (CH, 1024), 1)
    low = 8 * me + row
    if filter_order:
        high = 1023 - 8 * me - (row - 8)
    else:
        high = 1016 - 8 * me + (row - 8)
    chan = jnp.where(row < 8, low, high)
    if flipped:
        chan = 1023 - chan
    hit = lane == chan
    out = []
    for i in range(2):
        for k in range(3):
            w = sw_ref[k, i:i + 1, :]
            out.append(jnp.sum(jnp.where(hit, w, 0.0), axis=1, keepdims=True))
    return out


def wide(x):
    return jnp.broadcast_to(x, (CH, LN))[None]


STEP = 4
PIECES = 2
P_G, P_S, P_D, P_C, P_Q = 2, 1, 1, 1, 1
MESH = pl.DeviceIdType.MESH


def scatter(src, dst, send, recv):
    me = lax.axis_index("ctx")

    def one(o, _):
        q = lax.rem(me + o, NB)
        pltpu.make_async_remote_copy(
            src_ref=src.at[q], dst_ref=dst.at[me], send_sem=send, recv_sem=recv,
            device_id={"ctx": q}, device_id_type=MESH).start()
        return 0
    lax.fori_loop(1, NB, one, 0)
    dst[me] = src[me]


def await_all(ref, sem):
    part = ref.at[pl.ds(0, NB - 1)]
    pltpu.make_async_copy(part, part, sem).wait()


def to_chunks(get, dst):
    for j in range(4):
        low = get(j).T
        high = get(7 - j).T
        for g in range(16):
            both = jnp.concatenate([low[8 * g:8 * g + 8], high[120 - 8 * g:128 - 8 * g]], 0)
            dst[16 * j + g] = both.astype(BF)


def kernel(hid_h, cot_h, filt_h, sw_h, amat_h, bmat_h, tws_h, mats_h, mixed, gf, gs,
           hid, cot, filt, sw, amat, bmat, tws, mats,
           sendx, sendc, recvx, recvc, sendo, recvo,
           xrows, frows, qrows, conv_f, conv_r, gate_f, gate_r, buf, buf2,
           spec_s, spec_g, spec_d, tmp, tmp2, zs, zs2, half_out, half_in, pair_out, pair_in, small_in,
           sx, rx, sc, rc, so, ro, s2, r2, ins):
    pairs = ((hid_h, hid), (cot_h, cot), (filt_h, filt), (sw_h, sw), (amat_h, amat), (bmat_h, bmat), (tws_h, tws), (mats_h, mats))
    loads = [pltpu.make_async_copy(a, b, ins.at[i]) for i, (a, b) in enumerate(pairs)]
    for c in loads:
        c.start()
    me = lax.axis_index("ctx")
    dp = lax.axis_index("dp")
    core = lax.rem(dp, 2)
    yhi = dp // 2
    mate = yhi * 2 + 1 - core
    far = (1 - yhi) * 2 + core
    barrier = pltpu.get_barrier_semaphore()

    def greet(o, _):
        pl.semaphore_signal(barrier, inc=1, device_id={"ctx": lax.rem(me + o, NB)}, device_id_type=MESH)
        return 0
    lax.fori_loop(1, NB, greet, 0)
    for o in range(1, 4):
        pl.semaphore_signal(barrier, inc=1, device_id={"dp": lax.rem(dp + o, 4)}, device_id_type=MESH)

    every = list(range(CH))
    zero = jnp.zeros((CH, LN), F32)
    for p in (xrows, frows):
        p[0:CH] = zero
        p[(NB + 1) * CH:(NB + 2) * CH] = zero
    for h in range(2):
        qrows[h, 0:8] = zero[0:8]
        qrows[h, (NB + 1) * 8:(NB + 2) * 8] = zero[0:8]

    loads[0].wait()
    x = hid[...].astype(F32)
    scale = lax.rsqrt(jnp.mean(x * x, axis=1, keepdims=True) + 1e-06)
    to_chunks(lambda j: hid[:, j * LN:(j + 1) * LN].astype(F32) * scale, sendx)
    pl.semaphore_wait(barrier, NB - 1 + 3)
    scatter(sendx, recvx, sx, rx)
    loads[1].wait()
    to_chunks(lambda j: cot[:, j * LN:(j + 1) * LN].astype(F32), sendc)
    scatter(sendc, recvc, sc, rc)

    for c in loads[2:]:
        c.wait()
    wf = [wide(w) for w in tap_rows(sw, me, False, True)]
    wn = [wide(w) for w in tap_rows(sw, me, False, False)]
    wr = [wide(w) for w in tap_rows(sw, me, True, False)]

    for i in range(NB):
        frows[(i + 1) * CH:(i + 2) * CH] = filt[:, :, i * LN:(i + 1) * LN].astype(F32).reshape(CH, LN)

    def rows(i, more=0):
        return slice(i * STEP * CH, ((i + 1) * STEP + more) * CH)

    def tiles(ref, i, more=0):
        return ref[rows(i, more), :].reshape(STEP + more, CH, LN)

    for i in range(NB // STEP):
        v = tiles(frows, i, 2)
        g = wf[0] * shift(v, 0) + wf[1] * shift(v, 1) + wf[2] * shift(v, 2)
        buf[rows(i), :] = g.reshape(STEP * CH, LN)
    forward(buf, 0, spec_g, amat, tws, mats, zs, 0, every, False, P_G)

    await_all(recvx, rx)
    for i in range(NB):
        xrows[(i + 1) * CH:(i + 2) * CH] = recvx[i].astype(F32)
    forward(xrows, CH, spec_s, amat, tws, mats, zs, 0, every, True, P_S)

    for f in range(CH):
        r = row_f(f)
        gr, gi = halves(spec_g, f)
        sr, si = halves(spec_s, r)
        put(zs, r, gr * sr - gi * si, gr * si + gi * sr, P_C)
        sr, si = halves(spec_s, 15 - r)
        put(zs2, 15 - r, gr * sr + gi * si, gr * si - gi * sr, P_C)

    def keep(ref):
        def store(c, y):
            ref[column(c), :] = y
        return store
    inverse(zs, 0, CH, tmp, bmat, tws, mats, P_C, keep(conv_f))
    inverse(zs2, 0, CH, tmp2, bmat, tws, mats, P_C, keep(conv_r))
    for i in range(NB // STEP):
        v = tiles(xrows, i, 2)
        x0 = shift(v, 0)
        gf_ = wn[3] * x0 + wn[4] * shift(v, 1) + wn[5] * shift(v, 2)
        gr_ = wr[3] * x0 + wr[4] * shift(v, -1) + wr[5] * shift(v, -2)
        gate_f[rows(i), :] = gf_.reshape(STEP * CH, LN)
        gate_r[rows(i), :] = gr_.reshape(STEP * CH, LN)
        sendo[i * STEP:(i + 1) * STEP] = (gf_ * tiles(conv_f, i) + gr_ * tiles(conv_r, i)).astype(BF)
    scatter(sendo, recvo, so, ro)

    await_all(recvc, rc)
    for i in range(NB // STEP):
        ct = recvc[i * STEP:(i + 1) * STEP].astype(F32)
        buf[rows(i), :] = (ct * tiles(gate_f, i)).reshape(STEP * CH, LN)
        buf2[rows(i), :] = (ct * tiles(gate_r, i)).reshape(STEP * CH, LN)

    def q_half(h):
        own, other = every[8 * h:8 * h + 8], every[8 - 8 * h:16 - 8 * h]
        forward(buf, 0, spec_d, amat, tws, mats, zs, 0, own, False, P_D)
        forward(buf2, 0, spec_g, amat, tws, mats, zs, 8, other, False, P_D)
        for f in own:
            r = row_f(f)
            dr, di = halves(spec_d, r)
            sr, si = halves(spec_s, r)
            er, ei = halves(spec_g, 15 - r)
            tr, ti = halves(spec_s, 15 - r)
            put(zs2, f, dr * sr + di * si + er * tr + ei * ti, di * sr - dr * si + er * ti - ei * tr, P_Q)

        def store(f, y):
            qrows[h, column(f - 8 * h, 8, 8), :] = y
        inverse(zs2, 8 * h, 8, tmp, bmat, tws, mats, P_Q, store)
        for i in range(NB // STEP):
            v = qrows[h, i * STEP * 8:(i * STEP + STEP + 2) * 8, :].reshape(STEP + 2, 8, LN)
            g = 0.0
            for k in range(3):
                g = g + wf[k][:, 8 * h:8 * h + 8] * shift(v, -k)
            half_out[h, i * STEP:(i + 1) * STEP] = g

    for c in range(2):
        pl.when(core == c)(functools.partial(q_half, 1 - c))
    first = pltpu.make_async_remote_copy(
        src_ref=half_out.at[1 - core], dst_ref=half_in, send_sem=s2.at[0], recv_sem=r2.at[0],
        device_id={"dp": mate}, device_id_type=MESH)
    first.start()
    for c in range(2):
        pl.when(core == c)(functools.partial(q_half, c))
    first.wait()
    n = NB // 2 // PIECES
    seconds, thirds = [], []
    for p in range(PIECES):
        for i in range(p * n, (p + 1) * n):
            a = half_out[core, 2 * i:2 * i + 2] + half_in[2 * i:2 * i + 2]
            pair_out[i] = a.reshape(CH, LN).astype(BF)
        c = pltpu.make_async_remote_copy(
            src_ref=pair_out.at[pl.ds(p * n, n)], dst_ref=pair_in.at[pl.ds(p * n, n)],
            send_sem=s2.at[4 + p], recv_sem=r2.at[4 + p], device_id={"dp": far}, device_id_type=MESH)
        c.start()
        seconds.append(c)

    acc = [zero] * 9
    for i in range(NB // STEP):
        v = tiles(xrows, i, 2)
        ct = recvc[i * STEP:(i + 1) * STEP].astype(F32)
        cf = tiles(conv_f, i) * ct
        cr = tiles(conv_r, i) * ct
        fl = frows[(i * STEP + 1) * CH:((i + 1) * STEP + 1) * CH, :].reshape(STEP, CH, LN)
        q = jnp.concatenate([
            qrows[h, i * STEP * 8:(i * STEP + STEP + 2) * 8, :].reshape(STEP + 2, 8, LN) for h in range(2)], 1)
        for k in range(3):
            acc[k] = acc[k] + jnp.sum(fl * shift(q, -k), 0)
            acc[3 + k] = acc[3 + k] + jnp.sum(cf * shift(v, k), 0)
            acc[6 + k] = acc[6 + k] + jnp.sum(cr * shift(v, -k), 0)
    lane = lax.broadcasted_iota(jnp.int32, (CH, LN), 1)
    small = zero
    for k, a in enumerate(acc):
        small = jnp.where(lane == k, jnp.sum(a, 1, keepdims=True), small)
    small_in[dp] = small
    smalls = []
    for o in range(1, 4):
        c = pltpu.make_async_remote_copy(
            src_ref=small_in.at[dp], dst_ref=small_in.at[dp], send_sem=s2.at[o], recv_sem=r2.at[o],
            device_id={"dp": lax.rem(dp + o, 4)}, device_id_type=MESH)
        c.start()
        smalls.append(c)

    await_all(recvo, ro)
    for j in range(4):
        low = jnp.concatenate([recvo[16 * j + g].astype(F32)[0:8] for g in range(16)], 0)
        high = jnp.concatenate([recvo[16 * j + 15 - g].astype(F32)[8:16] for g in range(16)], 0)
        mixed[:, j * LN:(j + 1) * LN] = low.T.astype(BF)
        mixed[:, (7 - j) * LN:(8 - j) * LN] = high.T.astype(BF)

    for p in range(PIECES):
        seconds[p].wait()
        for i in range(p * n, (p + 1) * n):
            t = pair_out[i].astype(F32) + pair_in[i].astype(F32)
            gf[core, :, 2 * i * LN:(2 * i + 1) * LN] = t[0:8]
            gf[core, :, (2 * i + 1) * LN:(2 * i + 2) * LN] = t[8:16]
        part = gf.at[core, :, pl.ds(p * 2 * n * LN, 2 * n * LN)]
        c = pltpu.make_async_remote_copy(
            src_ref=part, dst_ref=part, send_sem=s2.at[4 + PIECES + p], recv_sem=r2.at[4 + PIECES + p],
            device_id={"dp": mate}, device_id_type=MESH)
        c.start()
        thirds.append(c)
    for c in smalls:
        c.wait()
    total = (small_in[0] + small_in[1]) + (small_in[2] + small_in[3])
    row = lax.broadcasted_iota(jnp.int32, (CH, LN), 0)

    def flat_rows(item, target):
        return jnp.sum(jnp.where(row == target, total[:, item:item + 1], 0.0), 0, keepdims=True)[:, 0:8]
    for k in range(3):
        gs[0, k] = jnp.concatenate([flat_rows(k, lane), flat_rows(k, lane + 8)], 0)
        gs[1, k] = jnp.concatenate([
            flat_rows(3 + k, lane) + flat_rows(6 + k, 15 - lane),
            flat_rows(3 + k, 15 - lane) + flat_rows(6 + k, lane)], 0)
    await_all(sendx, sx)
    await_all(sendc, sc)
    await_all(sendo, so)
    for c in thirds:
        c.wait()


def write(a, b, c, a_h, b_h, c_h, sems):
    copies = [pltpu.make_async_copy(x, y, sems.at[i]) for i, (x, y) in enumerate(((b, b_h), (a, a_h), (c, c_h)))]
    for x in copies:
        x.start()
    for x in copies:
        x.wait()


def run_kernel(hid, cot, filt, sw):
    amat, bmat, tws, mats = constants()
    vm = pl.BlockSpec(memory_space=pltpu.VMEM)
    dma = pltpu.SemaphoreType.DMA
    chunks = pltpu.VMEM((NB, CH, LN), BF)
    flat = pltpu.VMEM((NB * CH, LN), F32)
    padded = pltpu.VMEM(((NB + 2) * CH, LN), F32)
    spec = pltpu.VMEM((CH * NB, 2 * LN), F32)
    ops = (hid, cot, filt, sw, jnp.asarray(amat), jnp.asarray(bmat), jnp.asarray(tws), jnp.asarray(mats))
    held = [pltpu.VMEM(a.shape, a.dtype) for a in ops]
    outs = pl.pallas_call(
        kernel,
        out_shape=(
            pltpu.VMEM((LN, 1024), BF),
            pltpu.VMEM((2, 8, NB * LN), F32),
            pltpu.VMEM((2, 3, 2, 8), F32),
        ),
        in_specs=[pl.BlockSpec(memory_space=pltpu.HBM)] * 8,
        out_specs=(vm,) * 3,
        scratch_shapes=held + [chunks] * 6 + [padded] * 2 + [pltpu.VMEM((2, (NB + 2) * 8, LN), F32)] + [flat] * 6 + [spec] * 5 + [
            pltpu.VMEM((2, CH * NB, 2 * LN), BF),
            pltpu.VMEM((2, CH * NB, 2 * LN), BF),
            pltpu.VMEM((2, NB, 8, LN), F32),
            pltpu.VMEM((NB, 8, LN), F32),
            pltpu.VMEM((NB // 2, CH, LN), BF),
            pltpu.VMEM((NB // 2, CH, LN), BF),
            pltpu.VMEM((4, CH, LN), F32),
            dma, dma, dma, dma, dma, dma, dma((4 + 2 * PIECES,)), dma((4 + 2 * PIECES,)), dma((8,)),
        ],
        compiler_params=pltpu.CompilerParams(
            vmem_limit_bytes=57 << 20, collective_id=0, has_side_effects=True),
    )(*ops)
    return pl.pallas_call(
        write,
        out_shape=tuple(jax.ShapeDtypeStruct(a.shape, a.dtype) for a in outs),
        in_specs=[vm] * 3,
        out_specs=(pl.BlockSpec(memory_space=pltpu.HBM),) * 3,
        scratch_shapes=[dma((3,))],
        compiler_params=pltpu.CompilerParams(vmem_limit_bytes=1 << 20),
    )(*outs)


def local(hidden, sw, filt, cot):
    mixed, gf, gs = run_kernel(hidden[0], cot[0], filt, jnp.swapaxes(sw, 0, 1))
    return mixed[None], gf, gs


def solution(mesh):
    in_specs = (P("dp", "ctx", None), P(), P(None, "ctx", None), P("dp", "ctx", None))
    out_specs = (P("dp", "ctx", None), P(None, "ctx", None), P(None, None, None, "ctx"))
    return jax.shard_map(local, mesh=mesh, in_specs=in_specs, out_specs=out_specs, check_vma=False)
```

time: 41.3 us -> 39.3 us (0.952)
  local copies, waits for them, and re-layouts: 2.09 us -> 0 us
    unnamed x3 -> x0, local copies, waits for them, and re-layouts: 2.09 us -> none
    pallas_call x0 -> x1, Pallas kernels: none -> 0.91 us  [run_kernel(): pl.pallas_call(write, out_shape=tuple((jax.ShapeDtypeStruct(a.shape, a.dt...]
    pallas_call x1, Pallas kernels: 38.5 us -> 37.6 us  [run_kernel(): pl.pallas_call(kernel, out_shape=(pltpu.VMEM((LN, 1024), BF), pltpu.VMEM(...]
where the time goes in v3:
time: 39.3 us; the launch traced here: 39.2 us
  Pallas kernels  38.5 us (98%)
  between operations  0.64 us (2%)
    pallas_call x1, Pallas kernels, run_kernel(): pl.pallas_call(kernel, out_shape=(pltpu.VMEM((LN, 1024), BF), pltpu.VMEM(...  37.6 us
    pallas_call x1, Pallas kernels, run_kernel(): pl.pallas_call(write, out_shape=tuple((jax.ShapeDtypeStruct(a.shape, a.dt...  0.91 us

profile of v3, /device:TPU:1, one launch (start us, length us, event | category | flops | bytes accessed | tf_op | source)
XLA Modules:
  0.0 39.2 jit_solution(4476816007738851125)
XLA Ops:
  0.6 37.6 %shard_map.103 = (bf16[128,1024]{1,0:T(8,128)(2,1)S(1)}, f32[2,8,8192]{2,1,0:T(8,128)S(1)}, f32[2,3,2,8]{3,2,1,0:T(2,128)S(1)}) custom-call(bf16[128,1024]{1,0:T(8,128)(2,1)} %bitcast.4, bf16[128,1024]{1,0:T(8,128)(2,1)} %bitcast.5, bf16[2,8,8192]{2,1,0:T(8,128)(2,1)} %filt_h.1, f32[3,2,1024]{2,1,0:T(2,128)} %bitcast.6, ...), custom_call_target="tpu_custom_call" | custom-call | tf_op jit(solution)/shard_map/pallas_call | solution.py:417
  38.3 0.9 %shard_map.104 = (bf16[128,1024]{1,0:T(8,128)(2,1)}, f32[2,8,8192]{2,1,0:T(8,128)}, f32[2,3,2,8]{3,2,1,0:T(2,128)}) custom-call(bf16[128,1024]{1,0:T(8,128)(2,1)S(1)} %get-tuple-element.9.a, f32[2,8,8192]{2,1,0:T(8,128)S(1)} %get-tuple-element.10.b, f32[2,3,2,8]{3,2,1,0:T(2,128)S(1)} %get-tuple-element.11.c), custom_call_target="tpu_custom_call" | custom-call | tf_op jit(solution)/shard_map/pallas_call | solution.py:439

commit v4 on v3

v4 whole, which is shorter than its diff:
```python
import functools

import numpy as np, ml_dtypes
import jax, jax.numpy as jnp
from jax import lax
from jax.experimental import pallas as pl
from jax.experimental.pallas import tpu as pltpu
from jax.sharding import PartitionSpec as P

BF = jnp.bfloat16
F32 = jnp.float32
NB = 64
LN = 128
CH = 16
R = 8


def split(x):
    hi = x.astype(ml_dtypes.bfloat16)
    lo = (x - hi.astype(np.float64)).astype(ml_dtypes.bfloat16)
    return hi, lo


def constants():
    n = 2 * NB * LN
    k1 = np.arange(NB)[:, None] + 0.5
    n1 = np.arange(NB)[None, :]
    th = 2 * np.pi * k1 * n1 / LN
    a = np.concatenate([np.cos(th), -np.sin(th)], 0)
    b = np.concatenate([np.cos(th.T), -np.sin(th.T)], 1) * (2.0 / n)
    tw = 2 * np.pi * k1 * np.arange(LN)[None, :] / n
    twc, tws = np.cos(tw), np.sin(tw)
    ph = 2 * np.pi * np.outer(np.arange(LN), np.arange(LN)) / LN
    c, s = np.cos(ph), np.sin(ph)
    m = np.block([[c, -s], [s, c]])
    mi = np.block([[c, s], [-s, c]])
    ah, al = split(a)
    bh, bl = split(b)
    mh, ml = split(m)
    ih, il = split(mi)
    amat = np.concatenate([ah, ah, al], 1)
    bmat = np.concatenate([bh, bl], 1)
    tws = np.stack([twc, tws]).astype(np.float32)
    mats = np.stack([mh, ml, ih, il])
    return amat, bmat, tws, mats


def dot(a, b):
    return jnp.dot(a, b, preferred_element_type=F32)


def hilo(x):
    hi = x.astype(BF)
    return hi, (x - hi.astype(F32)).astype(BF)


ROW = ((0, 1, 2, 3, 7, 6, 5, 4), (3, 2, 1, 0, 4, 5, 6, 7))


def column(c, base=0):
    return pl.ds(base + c, NB, stride=R)


def shift(x, k):
    m = x.shape[0] - 2
    lane = lax.broadcasted_iota(jnp.int32, (1, 1, LN), 2)
    if k == 0:
        return x[1:m + 1]
    if k > 0:
        r = pltpu.roll(x[0:m + 1], k, 2)
        return jnp.where(lane < k, r[0:m], r[1:m + 1])
    r = pltpu.roll(x[1:m + 2], LN + k, 2)
    return jnp.where(lane >= LN + k, r[1:m + 1], r[0:m])


def forward(src, base, spec, to, amat, tws, mats, zs, exact, precise):
    twc, tws_ = tws[0], tws[1]
    for pair in range(R // 2):
        x = jnp.concatenate([src[column(c, base), :] for c in (2 * pair, 2 * pair + 1)], 1)
        hi, lo = hilo(x)
        if exact:
            p = dot(amat[:, 64:192], jnp.concatenate([hi, hi], 0))
        else:
            p = dot(amat[...], jnp.concatenate([hi, lo, hi], 0))
        for h in range(2):
            re = p[0:64, h * LN:(h + 1) * LN]
            im = p[64:128, h * LN:(h + 1) * LN]
            put(zs, to + 2 * pair + h, re * twc + im * tws_, im * twc - re * tws_, precise)
    big(zs, to * NB, spec, to * NB, R * NB, mats[0], mats[1], precise)


def big(zs, at, out, to, rows, mh, ml, precise):
    for r in range(0, rows, 256):
        zh = zs[0, at + r:at + r + 256, :]
        acc = dot(zh, mh)
        if precise > 0:
            acc = acc + dot(zh, ml)
        if precise > 1:
            acc = acc + dot(zs[1, at + r:at + r + 256, :], mh)
        out[to + r:to + r + 256, :] = acc


def put(zs, f, re, im, precise):
    z = jnp.concatenate([re, im], 1)
    zh, zl = hilo(z)
    zs[0, f * NB:(f + 1) * NB, :] = zh
    if precise > 1:
        zs[1, f * NB:(f + 1) * NB, :] = zl


def inverse(zs, slot, tmp, bmat, tws, mats, precise, store):
    big(zs, slot * NB, tmp, slot * NB, R * NB, mats[2], mats[3], precise)
    twc, tws_ = tws[0], tws[1]
    for pair in range(R // 2):
        us = []
        for h in range(2):
            r = (slot + 2 * pair + h) * NB
            re = tmp[r:r + NB, 0:LN]
            im = tmp[r:r + NB, LN:2 * LN]
            us.append(jnp.concatenate([re * twc - im * tws_, re * tws_ + im * twc], 0))
        u = jnp.concatenate(us, 1)
        uh, ul = hilo(u)
        y = dot(bmat[...], jnp.concatenate([uh, uh], 0))
        if precise > 1:
            y = y + dot(bmat[:, 0:128], ul)
        store(2 * pair, y[:, 0:LN])
        store(2 * pair + 1, y[:, LN:2 * LN])


def halves(ref, f):
    r = slice(f * NB, (f + 1) * NB)
    return ref[r, 0:LN], ref[r, LN:2 * LN]


def tap_rows(sw_ref, me, group, flipped, filter_order):
    row = lax.broadcasted_iota(jnp.int32, (R, 1024), 0)
    lane = lax.broadcasted_iota(jnp.int32, (R, 1024), 1)
    low = 8 * me + row
    high = 1016 - 8 * me + row
    if filter_order:
        high = 1016 - 8 * me + (11 - row if group == 0 else 3 - row)
    chan = jnp.where(row < 4, low, high) if group == 0 else jnp.where(row < 4, high, low)
    if flipped:
        chan = 1023 - chan
    hit = lane == chan
    out = []
    for i in range(2):
        for k in range(3):
            w = jnp.sum(jnp.where(hit, sw_ref[k, i:i + 1, :], 0.0), axis=1, keepdims=True)
            out.append(jnp.broadcast_to(w, (R, LN))[None])
    return out


STEP = 4
P_G, P_S, P_D, P_C, P_Q = 2, 1, 1, 1, 1
MESH = pl.DeviceIdType.MESH
HALF = NB // 2


def scatter(src, dst, send, recv):
    me = lax.axis_index("ctx")

    def one(o, _):
        q = lax.rem(me + o, NB)
        pltpu.make_async_remote_copy(
            src_ref=src.at[q], dst_ref=dst.at[me], send_sem=send, recv_sem=recv,
            device_id={"ctx": q}, device_id_type=MESH).start()
        return 0
    lax.fori_loop(1, NB, one, 0)
    dst[me] = src[me]


def await_all(ref, sem):
    part = ref.at[pl.ds(0, NB - 1)]
    pltpu.make_async_copy(part, part, sem).wait()


def kernel(hid_h, cot_h, filt_h, sw_h, amat_h, bmat_h, tws_h, mats_h, mixed, gf, gs,
           hid, cot, filt, sw, amat, bmat, tws, mats,
           sends, recvs, sendo, recvo,
           xrows, crows, frows, qrows, conv_f, conv_r, gate_f, gate_r, mixes, buf, buf2,
           spec_s, spec_g, spec_d, spec_e, tmp, tmp2, zs, zs2, half_out, half_in, pair_out, pair_in, small_in,
           ss, rs, so, ro, s2, r2, ins):
    pairs = ((hid_h, hid), (cot_h, cot), (filt_h, filt), (sw_h, sw), (amat_h, amat), (bmat_h, bmat), (tws_h, tws), (mats_h, mats))
    loads = [pltpu.make_async_copy(a, b, ins.at[i]) for i, (a, b) in enumerate(pairs)]
    for c in loads:
        c.start()
    me = lax.axis_index("ctx")
    dp = lax.axis_index("dp")
    core = lax.rem(dp, 2)
    yhi = dp // 2
    mate = yhi * 2 + 1 - core
    far = (1 - yhi) * 2 + core
    barrier = pltpu.get_barrier_semaphore()

    def greet(o, _):
        pl.semaphore_signal(barrier, inc=1, device_id={"ctx": lax.rem(me + o, NB)}, device_id_type=MESH)
        return 0
    lax.fori_loop(1, NB, greet, 0)
    for o in range(1, 4):
        pl.semaphore_signal(barrier, inc=1, device_id={"dp": lax.rem(dp + o, 4)}, device_id_type=MESH)

    zero = jnp.zeros((R, LN), F32)
    upper = lax.broadcasted_iota(jnp.int32, (R, LN), 0) < 4
    for g in range(2):
        for p in (xrows, frows, qrows):
            p[g, 0:R] = zero
            p[g, (NB + 1) * R:(NB + 2) * R] = zero

    loads[0].wait()
    x = hid[...].astype(F32)
    scale = lax.rsqrt(jnp.mean(x * x, axis=1, keepdims=True) + 1e-06)
    loads[1].wait()

    def block(j):
        at = slice(j * LN, (j + 1) * LN)
        return (hid[:, at].astype(F32) * scale).T, cot[:, at].astype(F32).T
    for j in range(4):
        low, high = block(j), block(7 - j)
        for i in range(16):
            a = [v[8 * i:8 * i + 8] for v in low]
            b = [v[120 - 8 * i:128 - 8 * i] for v in high]
            sends[0, 16 * j + i] = jnp.concatenate([jnp.where(upper, u, v) for u, v in zip(a, b)], 0).astype(BF)
            sends[1, 16 * j + i] = jnp.concatenate([jnp.where(upper, v, u) for u, v in zip(a, b)], 0).astype(BF)
    pl.semaphore_wait(barrier, NB - 1 + 3)
    for g in range(2):
        scatter(sends.at[g], recvs.at[g], ss.at[g], rs.at[g])

    for c in loads[2:]:
        c.wait()
    wf = [tap_rows(sw, me, g, False, True) for g in range(2)]
    wn = [tap_rows(sw, me, g, False, False) for g in range(2)]
    wr = [tap_rows(sw, me, g, True, False) for g in range(2)]

    def rows(i, more=0):
        return slice(i * STEP * R, ((i + 1) * STEP + more) * R)

    def tiles(ref, g, i, more=0):
        return ref[g, rows(i, more), :].reshape(STEP + more, R, LN)

    def flat(v):
        return v.reshape(STEP * R, LN)

    for i in range(NB):
        a = filt[0, :, i * LN:(i + 1) * LN].astype(F32)
        b = pltpu.roll(filt[1, :, i * LN:(i + 1) * LN].astype(F32), 4, 0)
        frows[0, (i + 1) * R:(i + 2) * R] = jnp.where(upper, a, b)
        frows[1, (i + 1) * R:(i + 2) * R] = jnp.where(upper, b, a)
    for g in range(2):
        for i in range(NB // STEP):
            v = tiles(frows, g, i, 2)
            buf[g, rows(i), :] = flat(wf[g][0] * shift(v, 0) + wf[g][1] * shift(v, 1) + wf[g][2] * shift(v, 2))
        forward(buf.at[g], 0, spec_g, g * R, amat, tws, mats, zs, False, P_G)

    def keep(ref, g, base=0):
        def store(c, y):
            ref[g, column(c, base), :] = y
        return store

    def outputs(g):
        await_all(recvs.at[g], rs.at[g])
        for i in range(NB):
            v = recvs[g, i].astype(F32)
            xrows[g, (i + 1) * R:(i + 2) * R] = v[0:R]
            crows[g, i * R:(i + 1) * R] = v[R:2 * R]
        forward(xrows.at[g], R, spec_s, g * R, amat, tws, mats, zs, True, P_S)
        for f in range(R):
            r = ROW[g][f]
            gr, gi = halves(spec_g, g * R + f)
            sr, si = halves(spec_s, g * R + r)
            put(zs, g * R + r, gr * sr - gi * si, gr * si + gi * sr, P_C)
            sr, si = halves(spec_s, g * R + 7 - r)
            put(zs2, g * R + 7 - r, gr * sr + gi * si, gr * si - gi * sr, P_C)
        inverse(zs, g * R, tmp, bmat, tws, mats, P_C, keep(conv_f, g))
        inverse(zs2, g * R, tmp2, bmat, tws, mats, P_C, keep(conv_r, g))
        n, r = wn[g], wr[g]
        for i in range(NB // STEP):
            v = tiles(xrows, g, i, 2)
            x0 = shift(v, 0)
            a = n[3] * x0 + n[4] * shift(v, 1) + n[5] * shift(v, 2)
            b = r[3] * x0 + r[4] * shift(v, -1) + r[5] * shift(v, -2)
            gate_f[g, rows(i), :] = flat(a)
            gate_r[g, rows(i), :] = flat(b)
            m = a * tiles(conv_f, g, i) + b * tiles(conv_r, g, i)
            if g == 0:
                mixes[0, rows(i), :] = flat(m)
            else:
                sendo[i * STEP:(i + 1) * STEP] = jnp.concatenate([tiles(mixes, 0, i), m], 1).astype(BF)

    def gradients(g):
        for i in range(NB // STEP):
            ct = tiles(crows, g, i)
            buf[g, rows(i), :] = flat(ct * tiles(gate_f, g, i))
            buf2[g, rows(i), :] = flat(ct * tiles(gate_r, g, i))
        forward(buf.at[g], 0, spec_d, g * R, amat, tws, mats, zs, False, P_D)
        forward(buf2.at[g], 0, spec_e, g * R, amat, tws, mats, zs2, False, P_D)
        for f in range(R):
            r = ROW[g][f]
            dr, di = halves(spec_d, g * R + r)
            sr, si = halves(spec_s, g * R + r)
            er, ei = halves(spec_e, g * R + 7 - r)
            tr, ti = halves(spec_s, g * R + 7 - r)
            put(zs, g * R + f, dr * sr + di * si + er * tr + ei * ti, di * sr - dr * si + er * ti - ei * tr, P_Q)
        inverse(zs, g * R, tmp, bmat, tws, mats, P_Q, keep(qrows, g, R))
        for i in range(NB // STEP):
            v = tiles(qrows, g, i, 2)
            half_out[g, i * STEP:(i + 1) * STEP] = sum(wf[g][k] * shift(v, -k) for k in range(3))
        c = pltpu.make_async_remote_copy(
            src_ref=half_out.at[g, pl.ds((1 - core) * HALF, HALF)], dst_ref=half_in.at[g],
            send_sem=s2.at[4 + g], recv_sem=r2.at[4 + g], device_id={"dp": mate}, device_id_type=MESH)
        c.start()
        return c

    def between_chips(g, first):
        first.wait()
        for i in range(HALF // 2):
            a = half_out[g, pl.ds(core * HALF + 2 * i, 2)] + half_in[g, 2 * i:2 * i + 2]
            pair_out[g, i] = a.reshape(CH, LN).astype(BF)
        c = pltpu.make_async_remote_copy(
            src_ref=pair_out.at[g], dst_ref=pair_in.at[g], send_sem=s2.at[6 + g], recv_sem=r2.at[6 + g],
            device_id={"dp": far}, device_id_type=MESH)
        c.start()
        return c

    def tap_sums(g):
        acc = [zero] * 9
        for i in range(NB // STEP):
            v = tiles(xrows, g, i, 2)
            ct = tiles(crows, g, i)
            cf = tiles(conv_f, g, i) * ct
            cr = tiles(conv_r, g, i) * ct
            fl = frows[g, (i * STEP + 1) * R:((i + 1) * STEP + 1) * R, :].reshape(STEP, R, LN)
            q = tiles(qrows, g, i, 2)
            for k in range(3):
                acc[k] = acc[k] + jnp.sum(fl * shift(q, -k), 0)
                acc[3 + k] = acc[3 + k] + jnp.sum(cf * shift(v, k), 0)
                acc[6 + k] = acc[6 + k] + jnp.sum(cr * shift(v, -k), 0)
        lane = lax.broadcasted_iota(jnp.int32, (R, LN), 1)
        small = zero
        for k, a in enumerate(acc):
            small = jnp.where(lane == k, jnp.sum(a, 1, keepdims=True), small)
        return small

    outputs(0)
    first0 = gradients(0)
    second0 = between_chips(0, first0)
    outputs(1)
    scatter(sendo, recvo, so, ro)
    first1 = gradients(1)
    small0 = tap_sums(0)
    second1 = between_chips(1, first1)
    small_in[dp] = jnp.concatenate([small0, tap_sums(1)], 0)
    smalls = []
    for o in range(1, 4):
        c = pltpu.make_async_remote_copy(
            src_ref=small_in.at[dp], dst_ref=small_in.at[dp], send_sem=s2.at[o], recv_sem=r2.at[o],
            device_id={"dp": lax.rem(dp + o, 4)}, device_id_type=MESH)
        c.start()
        smalls.append(c)

    await_all(recvo, ro)
    for j in range(4):
        low, high = [], []
        for i in range(16):
            v = recvo[16 * j + i].astype(F32)
            low.append(jnp.where(upper, v[0:R], v[R:2 * R]))
            high.append(jnp.where(upper, v[R:2 * R], v[0:R]))
        mixed[:, j * LN:(j + 1) * LN] = jnp.concatenate(low, 0).T.astype(BF)
        mixed[:, (7 - j) * LN:(8 - j) * LN] = jnp.concatenate(high[::-1], 0).T.astype(BF)

    second0.wait()
    second1.wait()
    for i in range(HALF // 2):
        a, b = [pair_out[g, i].astype(F32) + pair_in[g, i].astype(F32) for g in range(2)]
        for h in range(2):
            at = pl.ds(pl.multiple_of((core * HALF + 2 * i + h) * LN, LN), LN)
            u, v = a[R * h:R * h + R], b[R * h:R * h + R]
            gf[0, :, at] = jnp.where(upper, u, v)
            gf[1, :, at] = pltpu.roll(jnp.where(upper, v, u), 4, 0)
    part = gf.at[:, :, pl.ds(pl.multiple_of(core * HALF * LN, HALF * LN), HALF * LN)]
    third = pltpu.make_async_remote_copy(
        src_ref=part, dst_ref=part, send_sem=s2.at[0], recv_sem=r2.at[0],
        device_id={"dp": mate}, device_id_type=MESH)
    third.start()
    for c in smalls:
        c.wait()
    total = (small_in[0] + small_in[1]) + (small_in[2] + small_in[3])
    row = lax.broadcasted_iota(jnp.int32, (CH, LN), 0)
    lane = lax.broadcasted_iota(jnp.int32, (CH, LN), 1)
    near = jnp.where(lane < 4, lane, lane + 8)
    other = jnp.where(lane < 4, 7 - lane, 15 - lane)

    def pick(item, target):
        return jnp.sum(jnp.where(row == target, total[:, item:item + 1], 0.0), 0, keepdims=True)[:, 0:8]
    for k in range(3):
        gs[0, k] = jnp.concatenate([pick(k, near), pick(k, lane + 4)], 0)
        gs[1, k] = jnp.concatenate([pick(3 + k, near) + pick(6 + k, other), pick(3 + k, other) + pick(6 + k, near)], 0)
    for g in range(2):
        await_all(sends.at[g], ss.at[g])
    await_all(sendo, so)
    third.wait()


def write(a, b, c, a_h, b_h, c_h, sems):
    copies = [pltpu.make_async_copy(x, y, sems.at[i]) for i, (x, y) in enumerate(((b, b_h), (a, a_h), (c, c_h)))]
    for x in copies:
        x.start()
    for x in copies:
        x.wait()


def run_kernel(hid, cot, filt, sw):
    amat, bmat, tws, mats = constants()
    vm = pl.BlockSpec(memory_space=pltpu.VMEM)
    dma = pltpu.SemaphoreType.DMA
    def group(blocks, dtype=F32):
        return pltpu.VMEM((2, blocks * R, LN), dtype)
    chunks = pltpu.VMEM((NB, CH, LN), BF)
    both = pltpu.VMEM((2, NB, CH, LN), BF)
    spec = pltpu.VMEM((CH * NB, 2 * LN), F32)
    split_spec = pltpu.VMEM((2, CH * NB, 2 * LN), BF)
    ops = (hid, cot, filt, sw, jnp.asarray(amat), jnp.asarray(bmat), jnp.asarray(tws), jnp.asarray(mats))
    held = [pltpu.VMEM(a.shape, a.dtype) for a in ops]
    outs = pl.pallas_call(
        kernel,
        out_shape=(
            pltpu.VMEM((LN, 1024), BF),
            pltpu.VMEM((2, 8, NB * LN), F32),
            pltpu.VMEM((2, 3, 2, 8), F32),
        ),
        in_specs=[pl.BlockSpec(memory_space=pltpu.HBM)] * 8,
        out_specs=(vm,) * 3,
        scratch_shapes=held + [both] * 2 + [chunks] * 2 + [
            group(NB + 2), group(NB), group(NB + 2), group(NB + 2)] + [group(NB)] * 7 + [spec] * 6 + [split_spec] * 2 + [
            pltpu.VMEM((2, NB, R, LN), F32),
            pltpu.VMEM((2, HALF, R, LN), F32),
            pltpu.VMEM((2, HALF // 2, CH, LN), BF),
            pltpu.VMEM((2, HALF // 2, CH, LN), BF),
            pltpu.VMEM((4, CH, LN), F32),
            dma((2,)), dma((2,)), dma, dma, dma((8,)), dma((8,)), dma((8,)),
        ],
        compiler_params=pltpu.CompilerParams(
            vmem_limit_bytes=57 << 20, collective_id=0, has_side_effects=True),
    )(*ops)
    return pl.pallas_call(
        write,
        out_shape=tuple(jax.ShapeDtypeStruct(a.shape, a.dtype) for a in outs),
        in_specs=[vm] * 3,
        out_specs=(pl.BlockSpec(memory_space=pltpu.HBM),) * 3,
        scratch_shapes=[dma((3,))],
        compiler_params=pltpu.CompilerParams(vmem_limit_bytes=1 << 20),
    )(*outs)


def local(hidden, sw, filt, cot):
    mixed, gf, gs = run_kernel(hidden[0], cot[0], filt, jnp.swapaxes(sw, 0, 1))
    return mixed[None], gf, gs


def solution(mesh):
    in_specs = (P("dp", "ctx", None), P(), P(None, "ctx", None), P("dp", "ctx", None))
    out_specs = (P("dp", "ctx", None), P(None, "ctx", None), P(None, None, None, "ctx"))
    return jax.shard_map(local, mesh=mesh, in_specs=in_specs, out_specs=out_specs, check_vma=False)
```

time: 39.3 us -> 42 us (1.069)
  Pallas kernels: 38.5 us -> 41.3 us
    pallas_call x1, Pallas kernels: 37.6 us -> 40.4 us  [run_kernel(): pl.pallas_call(kernel, out_shape=(pltpu.VMEM((LN, 1024), BF), pltpu.VMEM(...]
where the time goes in v4:
time: 42 us
  Pallas kernels  41.3 us (98%)
  between operations  0.64 us (2%)
    pallas_call x1, Pallas kernels, run_kernel(): pl.pallas_call(kernel, out_shape=(pltpu.VMEM((LN, 1024), BF), pltpu.VMEM(...  40.4 us
    pallas_call x1, Pallas kernels, run_kernel(): pl.pallas_call(write, out_shape=tuple((jax.ShapeDtypeStruct(a.shape, a.dt...  0.91 us

profile of v4, /device:TPU:1, one launch (start us, length us, event | category | flops | bytes accessed | tf_op | source)
XLA Modules:
  0.0 42.0 jit_solution(14238948907529354854)
XLA Ops:
  0.6 40.4 %shard_map.103 = (bf16[128,1024]{1,0:T(8,128)(2,1)S(1)}, f32[2,8,8192]{2,1,0:T(8,128)S(1)}, f32[2,3,2,8]{3,2,1,0:T(2,128)S(1)}) custom-call(bf16[128,1024]{1,0:T(8,128)(2,1)} %bitcast.4, bf16[128,1024]{1,0:T(8,128)(2,1)} %bitcast.5, bf16[2,8,8192]{2,1,0:T(8,128)(2,1)} %filt_h.1, f32[3,2,1024]{2,1,0:T(2,128)} %bitcast.6, ...), custom_call_target="tpu_custom_call" | custom-call | tf_op jit(solution)/shard_map/pallas_call | solution.py:424
  41.0 0.9 %shard_map.104 = (bf16[128,1024]{1,0:T(8,128)(2,1)}, f32[2,8,8192]{2,1,0:T(8,128)}, f32[2,3,2,8]{3,2,1,0:T(2,128)}) custom-call(bf16[128,1024]{1,0:T(8,128)(2,1)S(1)} %get-tuple-element.9.a, f32[2,8,8192]{2,1,0:T(8,128)S(1)} %get-tuple-element.10.b, f32[2,3,2,8]{3,2,1,0:T(2,128)S(1)} %get-tuple-element.11.c), custom_call_target="tpu_custom_call" | custom-call | tf_op jit(solution)/shard_map/pallas_call | solution.py:445

commit v5 on v3

--- a/solution.py
+++ b/solution.py
@@ -157,7 +157,7 @@
 
 
 STEP = 4
-PIECES = 2
+PIECES = 4
 P_G, P_S, P_D, P_C, P_Q = 2, 1, 1, 1, 1
 MESH = pl.DeviceIdType.MESH
 
@@ -171,7 +171,7 @@
             src_ref=src.at[q], dst_ref=dst.at[me], send_sem=send, recv_sem=recv,
             device_id={"ctx": q}, device_id_type=MESH).start()
         return 0
-    lax.fori_loop(1, NB, one, 0)
+    lax.fori_loop(1, NB, one, 0, unroll=9)
     dst[me] = src[me]
 
 
@@ -193,7 +193,7 @@
            hid, cot, filt, sw, amat, bmat, tws, mats,
            sendx, sendc, recvx, recvc, sendo, recvo,
            xrows, frows, qrows, conv_f, conv_r, gate_f, gate_r, buf, buf2,
-           spec_s, spec_g, spec_d, tmp, tmp2, zs, zs2, half_out, half_in, pair_out, pair_in, small_in,
+           spec_s, spec_g, spec_d, tmp, tmp2, zs, zs2, half_out, half_send, half_in, pair_out, pair_in, small_in,
            sx, rx, sc, rc, so, ro, s2, r2, ins):
     pairs = ((hid_h, hid), (cot_h, cot), (filt_h, filt), (sw_h, sw), (amat_h, amat), (bmat_h, bmat), (tws_h, tws), (mats_h, mats))
     loads = [pltpu.make_async_copy(a, b, ins.at[i]) for i, (a, b) in enumerate(pairs)]
@@ -210,7 +210,7 @@
     def greet(o, _):
         pl.semaphore_signal(barrier, inc=1, device_id={"ctx": lax.rem(me + o, NB)}, device_id_type=MESH)
         return 0
-    lax.fori_loop(1, NB, greet, 0)
+    lax.fori_loop(1, NB, greet, 0, unroll=9)
     for o in range(1, 4):
         pl.semaphore_signal(barrier, inc=1, device_id={"dp": lax.rem(dp + o, 4)}, device_id_type=MESH)
 
@@ -284,13 +284,14 @@
     scatter(sendo, recvo, so, ro)
 
     await_all(recvc, rc)
-    for i in range(NB // STEP):
-        ct = recvc[i * STEP:(i + 1) * STEP].astype(F32)
-        buf[rows(i), :] = (ct * tiles(gate_f, i)).reshape(STEP * CH, LN)
-        buf2[rows(i), :] = (ct * tiles(gate_r, i)).reshape(STEP * CH, LN)
-
-    def q_half(h):
+    def q_half(h, mine):
         own, other = every[8 * h:8 * h + 8], every[8 - 8 * h:16 - 8 * h]
+        for i in range(NB):
+            ct = recvc[i].astype(F32)
+            u = slice(i * CH + 8 * h, i * CH + 8 * h + 8)
+            v = slice(i * CH + 8 - 8 * h, i * CH + 16 - 8 * h)
+            buf[u, :] = ct[8 * h:8 * h + 8] * gate_f[u, :]
+            buf2[v, :] = ct[8 - 8 * h:16 - 8 * h] * gate_r[v, :]
         forward(buf, 0, spec_d, amat, tws, mats, zs, 0, own, False, P_D)
         forward(buf2, 0, spec_g, amat, tws, mats, zs, 8, other, False, P_D)
         for f in own:
@@ -309,23 +310,26 @@
             g = 0.0
             for k in range(3):
                 g = g + wf[k][:, 8 * h:8 * h + 8] * shift(v, -k)
-            half_out[h, i * STEP:(i + 1) * STEP] = g
+            g = g.reshape(STEP // 2, CH, LN)
+            if mine:
+                half_out[i * STEP // 2:(i + 1) * STEP // 2] = g
+            else:
+                half_send[i * STEP // 2:(i + 1) * STEP // 2] = g.astype(BF)
 
     for c in range(2):
-        pl.when(core == c)(functools.partial(q_half, 1 - c))
+        pl.when(core == c)(functools.partial(q_half, 1 - c, False))
     first = pltpu.make_async_remote_copy(
-        src_ref=half_out.at[1 - core], dst_ref=half_in, send_sem=s2.at[0], recv_sem=r2.at[0],
+        src_ref=half_send, dst_ref=half_in, send_sem=s2.at[0], recv_sem=r2.at[0],
         device_id={"dp": mate}, device_id_type=MESH)
     first.start()
     for c in range(2):
-        pl.when(core == c)(functools.partial(q_half, c))
+        pl.when(core == c)(functools.partial(q_half, c, True))
     first.wait()
     n = NB // 2 // PIECES
     seconds, thirds = [], []
     for p in range(PIECES):
         for i in range(p * n, (p + 1) * n):
-            a = half_out[core, 2 * i:2 * i + 2] + half_in[2 * i:2 * i + 2]
-            pair_out[i] = a.reshape(CH, LN).astype(BF)
+            pair_out[i] = (half_out[i] + half_in[i].astype(F32)).astype(BF)
         c = pltpu.make_async_remote_copy(
             src_ref=pair_out.at[pl.ds(p * n, n)], dst_ref=pair_in.at[pl.ds(p * n, n)],
             send_sem=s2.at[4 + p], recv_sem=r2.at[4 + p], device_id={"dp": far}, device_id_type=MESH)
@@ -358,13 +362,6 @@
         c.start()
         smalls.append(c)
 
-    await_all(recvo, ro)
-    for j in range(4):
-        low = jnp.concatenate([recvo[16 * j + g].astype(F32)[0:8] for g in range(16)], 0)
-        high = jnp.concatenate([recvo[16 * j + 15 - g].astype(F32)[8:16] for g in range(16)], 0)
-        mixed[:, j * LN:(j + 1) * LN] = low.T.astype(BF)
-        mixed[:, (7 - j) * LN:(8 - j) * LN] = high.T.astype(BF)
-
     for p in range(PIECES):
         seconds[p].wait()
         for i in range(p * n, (p + 1) * n):
@@ -377,6 +374,14 @@
             device_id={"dp": mate}, device_id_type=MESH)
         c.start()
         thirds.append(c)
+
+    await_all(recvo, ro)
+    for j in range(4):
+        low = jnp.concatenate([recvo[16 * j + g].astype(F32)[0:8] for g in range(16)], 0)
+        high = jnp.concatenate([recvo[16 * j + 15 - g].astype(F32)[8:16] for g in range(16)], 0)
+        mixed[:, j * LN:(j + 1) * LN] = low.T.astype(BF)
+        mixed[:, (7 - j) * LN:(8 - j) * LN] = high.T.astype(BF)
+
     for c in smalls:
         c.wait()
     total = (small_in[0] + small_in[1]) + (small_in[2] + small_in[3])
@@ -426,8 +431,9 @@
         scratch_shapes=held + [chunks] * 6 + [padded] * 2 + [pltpu.VMEM((2, (NB + 2) * 8, LN), F32)] + [flat] * 6 + [spec] * 5 + [
             pltpu.VMEM((2, CH * NB, 2 * LN), BF),
             pltpu.VMEM((2, CH * NB, 2 * LN), BF),
-            pltpu.VMEM((2, NB, 8, LN), F32),
-            pltpu.VMEM((NB, 8, LN), F32),
+            pltpu.VMEM((NB // 2, CH, LN), F32),
+            pltpu.VMEM((NB // 2, CH, LN), BF),
+            pltpu.VMEM((NB // 2, CH, LN), BF),
             pltpu.VMEM((NB // 2, CH, LN), BF),
             pltpu.VMEM((NB // 2, CH, LN), BF),
             pltpu.VMEM((4, CH, LN), F32),

time: 39.3 us -> 39 us (level)
  no operation moved by 1% of the time
where the time goes in v5:
time: 39 us; the launch traced here: 38.9 us
  Pallas kernels  38.3 us (98%)
  between operations  0.64 us (2%)
    pallas_call x1, Pallas kernels, run_kernel(): pl.pallas_call(kernel, out_shape=(pltpu.VMEM((LN, 1024), BF), pltpu.VMEM(...  37.4 us
    pallas_call x1, Pallas kernels, run_kernel(): pl.pallas_call(write, out_shape=tuple((jax.ShapeDtypeStruct(a.shape, a.dt...  0.91 us

profile of v5, /device:TPU:1, one launch (start us, length us, event | category | flops | bytes accessed | tf_op | source)
XLA Modules:
  0.0 38.9 jit_solution(6213260223997855839)
XLA Ops:
  0.6 37.4 %shard_map.103 = (bf16[128,1024]{1,0:T(8,128)(2,1)S(1)}, f32[2,8,8192]{2,1,0:T(8,128)S(1)}, f32[2,3,2,8]{3,2,1,0:T(2,128)S(1)}) custom-call(bf16[128,1024]{1,0:T(8,128)(2,1)} %bitcast.4, bf16[128,1024]{1,0:T(8,128)(2,1)} %bitcast.5, bf16[2,8,8192]{2,1,0:T(8,128)(2,1)} %filt_h.1, f32[3,2,1024]{2,1,0:T(2,128)} %bitcast.6, ...), custom_call_target="tpu_custom_call" | custom-call | tf_op jit(solution)/shard_map/pallas_call | solution.py:422
  38.0 0.9 %shard_map.104 = (bf16[128,1024]{1,0:T(8,128)(2,1)}, f32[2,8,8192]{2,1,0:T(8,128)}, f32[2,3,2,8]{3,2,1,0:T(2,128)}) custom-call(bf16[128,1024]{1,0:T(8,128)(2,1)S(1)} %get-tuple-element.9.a, f32[2,8,8192]{2,1,0:T(8,128)S(1)} %get-tuple-element.10.b, f32[2,3,2,8]{3,2,1,0:T(2,128)S(1)} %get-tuple-element.11.c), custom_call_target="tpu_custom_call" | custom-call | tf_op jit(solution)/shard_map/pallas_call | solution.py:445
